TPU v7x, 128 devices: a whole 4x4x4 slice. The times are simulated.
128 devices in a mesh: lat: 4 (over y_hi, core), lon: 32 (over z, x, y_lo).
Axes of the slice: x: 4, y: 4 (y_hi: 2, y_lo: 2; y = y_hi * 2 + y_lo), z: 4, core: 2. Of those that a mesh axis runs over, the one named last changes fastest.
Arguments:
- tokens: bfloat16 [2, 24, 1536, 192], P(None, 'lat', 'lon'), may hold values from -6 to 6
- cotangent: bfloat16 [2, 24, 1536, 192], P(None, 'lat', 'lon'), may hold values from -6 to 6
- norm_gains: float32 [2, 2, 192], replicated, may hold values from 0.1 to 1.9
- w_qkv: bfloat16 [2, 192, 576], replicated, may hold values from -0.4375 to 0.4375
- w_proj: bfloat16 [2, 192, 192], replicated, may hold values from -0.4375 to 0.4375
- w_up: bfloat16 [2, 192, 768], replicated, may hold values from -0.4375 to 0.4375
- w_down: bfloat16 [2, 768, 192], replicated, may hold values from -0.21875 to 0.21875
- pos_bias: float32 [2, 6, 144, 144], replicated, may hold values from -4 to 300
Outputs:
- grad_input: bfloat16 [2, 24, 1536, 192], P(None, 'lat', 'lon')
- grad_matrix: float32 [2, 192, 2304], P(None, None, ('lat', 'lon'))
- grad_other: float32 [2, 124800], P(None, ('lat', 'lon'))
All inputs are finite; a program needn't handle non-finite values.
Results may differ from a plain program's by a relative error of at most 0.03.
Values may be sent and summed in bfloat16 or wider, within the bound.
A program may use at most 128 MiB of HBM per device.

v0:
```python
import math

import jax
import jax.numpy as jnp
from jax import lax
from jax.sharding import PartitionSpec as P

C = 192
HEADS = 6
WLAT = 6
WLON = 12
SLAT = 3
SLON = 6
VECB = 124800


def padded(cells, sides, width, closed):
    for axis, dim in sides:
        count = lax.axis_size(axis)
        ends = count if closed else count - 1
        head = lax.slice_in_dim(cells, 0, width, axis=dim)
        tail = lax.slice_in_dim(cells, cells.shape[dim] - width, cells.shape[dim], axis=dim)
        cells = jnp.concatenate(
            [
                lax.ppermute(tail, axis, [(i, (i + 1) % count) for i in range(ends)]),
                cells,
                lax.ppermute(head, axis, [((i + 1) % count, i) for i in range(ends)]),
            ],
            axis=dim,
        )
    return cells


def layer_norm(values, gain_vec):
    widened = values.astype(jnp.float32)
    center = widened - jnp.mean(widened, axis=-1, keepdims=True)
    spread = jnp.mean(center * center, axis=-1, keepdims=True)
    return (center * lax.rsqrt(spread + 1e-05) * gain_vec).astype(jnp.bfloat16)


def to_windows(grid_field):
    levels, lat_rows, lon_cols, channels = grid_field.shape
    blocks_view = grid_field.reshape(
        levels, lat_rows // WLAT, WLAT, lon_cols // WLON, WLON, channels
    )
    blocks_view = blocks_view.transpose(1, 3, 0, 2, 4, 5)
    return blocks_view.reshape(
        lat_rows // WLAT * (lon_cols // WLON), levels * WLAT * WLON, channels
    )


def from_windows(windows, levels, lat_rows, lon_cols):
    channels = windows.shape[-1]
    blocks_view = windows.reshape(lat_rows // WLAT, lon_cols // WLON, levels, WLAT, WLON, channels)
    return blocks_view.transpose(2, 0, 3, 1, 4, 5).reshape(levels, lat_rows, lon_cols, channels)


def window_attention(normed, w_qkv, w_proj, bias_table, keys_kept):
    window_count, tokens_win, channels = normed.shape
    head_size = channels // HEADS
    packed = jnp.dot(
        normed.reshape(window_count * tokens_win, channels),
        w_qkv,
        preferred_element_type=jnp.float32,
    )
    packed = lax.optimization_barrier(packed.astype(jnp.bfloat16)).astype(jnp.float32)
    packed = packed.reshape(window_count, tokens_win, 3, HEADS, head_size)
    scores = (
        jnp.einsum("nqhd,nkhd->nhqk", packed[:, :, 0], packed[:, :, 1]) * head_size ** (-0.5)
        + bias_table[None]
    )
    scores = jnp.where(keys_kept[:, None, None, :], scores, -1e30)
    weights = jax.nn.softmax(scores, axis=-1)
    weights = lax.optimization_barrier(weights.astype(jnp.bfloat16)).astype(jnp.float32)
    mixed_heads = jnp.einsum("nhqk,nkhd->nqhd", weights, packed[:, :, 2]).astype(jnp.bfloat16)
    result = jnp.dot(
        mixed_heads.reshape(window_count * tokens_win, channels),
        w_proj,
        preferred_element_type=jnp.float32,
    )
    return result.astype(jnp.bfloat16).reshape(window_count, tokens_win, channels)


def feed_forward(hidden, gain_vec, w_up, w_down):
    in_shape = hidden.shape
    normed = layer_norm(hidden, gain_vec).reshape(-1, in_shape[-1])
    inner_act = jax.nn.gelu(
        jnp.dot(normed, w_up, preferred_element_type=jnp.float32), approximate=False
    )
    inner_act = inner_act.astype(jnp.bfloat16)
    result = jnp.dot(inner_act, w_down, preferred_element_type=jnp.float32).reshape(in_shape)
    return (hidden + result).astype(jnp.bfloat16)


def plain_block(tokens, gains, w_qkv, w_proj, w_up, w_down, bias_table):
    levels, lat_rows, lon_cols, channels = tokens.shape
    normed = to_windows(layer_norm(tokens, gains[0]))
    keys_kept = jnp.ones(normed.shape[:2], dtype=bool)
    attended = from_windows(
        window_attention(normed, w_qkv, w_proj, bias_table, keys_kept), levels, lat_rows, lon_cols
    )
    hidden = tokens.astype(jnp.float32) + attended.astype(jnp.float32)
    return feed_forward(hidden, gains[1], w_up, w_down)


def widen(grid_field):
    with_cols = padded(grid_field, (("lon", 2),), SLON, True)
    return padded(with_cols, (("lat", 1),), SLAT, False)


def pack_grads(grad_qkv, grad_proj, grad_up, grad_down, grad_bias, gain_norm, gain_feed):
    matrix = jnp.concatenate(
        [
            grad_qkv.astype(jnp.float32),
            grad_proj.astype(jnp.float32),
            grad_up.astype(jnp.float32),
            grad_down.T.astype(jnp.float32),
        ],
        axis=1,
    )
    remainder = jnp.concatenate([grad_bias.reshape(-1), gain_norm, gain_feed])
    return (matrix, remainder)


def shards(tokens, cotangent, norm_gains, w_qkv, w_proj, w_up, w_down, pos_bias):
    levels, lat_rows, lon_cols, channels = tokens.shape
    after_first, pull_first = jax.vjp(
        plain_block, tokens, norm_gains[0], w_qkv[0], w_proj[0], w_up[0], w_down[0], pos_bias[0]
    )
    normed, pull_norm = jax.vjp(layer_norm, after_first, norm_gains[1, 0])
    band_index = lax.axis_index("lat")
    band_total = lax.axis_size("lat")
    widened = widen(normed)
    ext_rows = lat_rows + 2 * SLAT
    ext_cols = lon_cols + 2 * SLON
    row_index = (
        lax.broadcasted_iota(jnp.int32, (levels, ext_rows, ext_cols, 1), 1)
        + band_index * lat_rows
        - SLAT
    )
    keys_kept = to_windows((row_index >= 0) & (row_index < band_total * lat_rows))[..., 0]
    row_pos = jnp.arange(ext_rows // WLAT)
    col_pos = jnp.arange(ext_cols // WLON)
    lat_count = (
        1
        + ((row_pos == 0) & (band_index > 0)).astype(jnp.int32)
        + ((row_pos == ext_rows // WLAT - 1) & (band_index < band_total - 1)).astype(jnp.int32)
    )
    lon_count = (
        1 + (col_pos == 0).astype(jnp.int32) + (col_pos == ext_cols // WLON - 1).astype(jnp.int32)
    )
    window_copies = (lat_count[:, None] * lon_count[None, :]).reshape(-1, 1, 1)
    copy_counts = window_copies.astype(jnp.bfloat16)
    copy_shares = (1.0 / window_copies.astype(jnp.float32)).astype(jnp.bfloat16)

    def shifted_attention(windows, qkv_weight, proj_weight, bias_table):
        return window_attention(windows, qkv_weight, proj_weight, bias_table, keys_kept)

    attended_win, pull_shift = jax.vjp(
        shifted_attention, to_windows(widened), w_qkv[1], w_proj[1], pos_bias[1]
    )
    attended = from_windows(attended_win, levels, ext_rows, ext_cols)[
        :, SLAT : SLAT + lat_rows, SLON : SLON + lon_cols
    ]
    hidden = after_first.astype(jnp.float32) + attended.astype(jnp.float32)
    _, pull_feed = jax.vjp(feed_forward, hidden, norm_gains[1, 1], w_up[1], w_down[1])
    grad_hidden, gain_feed_two, up_two, down_two = pull_feed(cotangent)
    grad_attended = grad_hidden.astype(jnp.bfloat16)
    grad_windows = to_windows(widen(grad_attended))
    grad_inputs, qkv_grad, proj_grad, bias_grad = pull_shift(grad_windows * copy_shares)
    grad_normed = from_windows(grad_inputs * copy_counts, levels, ext_rows, ext_cols)
    grad_normed, qkv_two, proj_two, bias_two = (
        grad_normed[:, SLAT : SLAT + lat_rows, SLON : SLON + lon_cols],
        qkv_grad,
        proj_grad,
        bias_grad,
    )
    grad_from_norm, gain_norm_two = pull_norm(grad_normed)
    grad_after_first = grad_from_norm + grad_attended
    second_grads = pack_grads(
        qkv_two, proj_two, up_two, down_two, bias_two, gain_norm_two, gain_feed_two
    )
    grad_tokens, gains_one, qkv_one, proj_one, up_one, down_one, bias_one = pull_first(
        grad_after_first
    )
    first_grads = pack_grads(
        qkv_one, proj_one, up_one, down_one, bias_one, gains_one[0], gains_one[1]
    )
    matrix, remainder = (
        lax.psum_scatter(
            jnp.stack([first_grads[0], second_grads[0]]),
            ("lat", "lon"),
            scatter_dimension=2,
            tiled=True,
        ),
        lax.psum_scatter(
            jnp.stack([first_grads[1], second_grads[1]]),
            ("lat", "lon"),
            scatter_dimension=1,
            tiled=True,
        ),
    )
    sum_squares = lax.psum(
        jnp.sum(matrix * matrix) + jnp.sum(remainder * remainder), ("lat", "lon")
    )
    ceiling = math.sqrt(24 * C * C + 2 * VECB)
    factor = jnp.minimum(1.0, ceiling / (jnp.sqrt(sum_squares) + 1e-06))
    return (grad_tokens, matrix * factor, remainder * factor)


def solution(mesh):
    return jax.shard_map(
        shards,
        mesh=mesh,
        in_specs=(
            P(None, "lat", "lon", None),
            P(None, "lat", "lon", None),
            P(),
            P(),
            P(),
            P(),
            P(),
            P(),
        ),
        out_specs=(
            P(None, "lat", "lon", None),
            P(None, None, ("lat", "lon")),
            P(None, ("lat", "lon")),
        ),
        check_vma=False,
    )
```

profile of v0, /device:TPU:1, one launch (start us, length us, event | category | flops | bytes accessed | tf_op | source)
XLA Modules:
  0.0 531.9 jit_solution(17471096557979002262)
XLA Ops:
  36.9 5.3 %multiply_convert_fusion.1 = (bf16[576,768]{1,0:T(8,128)(2,1)S(1)}, f32[576,768]{1,0:T(8,128)}, f32[576,768]{1,0:T(8,128)}) fusion(bf16[576,192]{1,0:T(8,128)(2,1)S(1)} %bitcast.248, bf16[2,192,768]{2,1,0:T(8,128)(2,1)S(1)} %copy-done.60), kind=kOutput, calls=%fused_computation.78 | convolution fusion | flops 198623232 | bytes 5013504 | tf_op jit(solution)/shard_map/jvp()/dot_general | solution.py:88
  46.8 5.7 %collective-permute-start.1 = (bf16[2,6,6,192]{3,2,1,0:T(8,128)(2,1)}, bf16[2,6,6,192]{3,2,1,0:T(8,128)(2,1)}, u32[]{:S(2)}, u32[]{:S(2)}) collective-permute-start(bf16[2,6,6,192]{3,2,1,0:T(8,128)(2,1)} %get-tuple-element.40), channel_id=1, source_target_pairs={{1,0},{2,1},{3,2},{4,3},{5,4},{6,5},{7,6},{8,7},{9,8},{10,9},{11,1... | collective-permute-start | bytes 82952 | tf_op jit(solution)/shard_map/ppermute | solution.py:27
  57.6 2.5 copy.155
  61.3 5.4 %collective-permute-start.2 = (bf16[2,3,60,192]{3,2,1,0:T(8,128)(2,1)S(1)}, bf16[2,3,60,192]{3,2,1,0:T(8,128)(2,1)S(1)}, u32[]{:S(2)}, u32[]{:S(2)}) collective-permute-start(bf16[2,3,60,192]{3,2,1,0:T(8,128)(2,1)S(1)} %get-tuple-element.35), channel_id=1, source_target_pairs={{0,32},{32,64},{64,96},{1,33},{33,65},{65,97},{2,34},{34,66},{66,9... | collective-permute-start | bytes 414728 | tf_op jit(solution)/shard_map/ppermute | solution.py:25
  66.7 2.4 collective-permute-start.3
  70.4 4.8 collective-permute-done.3
  80.4 3.1 convolution_convert_fusion
  83.5 8.7 %reshape.335 = bf16[10,144,3,6,32]{1,0,4,3,2:T(8,128)(2,1)} reshape(bf16[1440,576]{0,1:T(8,128)(2,1)} %convolution_convert_fusion) | data formatting | bytes 3317760 | tf_op jit(solution)/shard_map/jvp()/reshape | solution.py:67
  92.1 4.7 fusion.167
  96.8 11.1 %fusion.176 = (f32[10,6,144]{2,1,0:T(8,128)}, f32[10,6,144,144]{2,3,1,0:T(8,128)}) fusion(f32[6,144,144]{1,2,0:T(8,128)} %copy.155, pred[10,144]{1,0:T(8,128)(4,1)} %transpose.117, bf16[10,144,1,6,32]{1,0,4,3,2:T(8,128)(2,1)} %get-tuple-element.26, bf16[10,144,1,6,32]{1,0,4,3,2:T(8,128)(2,1)} %get-tuple-element.27), kind=kOutput, calls=%fused_computation.298 | convolution fusion | flops 85847184 | bytes 6616224 | tf_op jit(solution)/shard_map/jvp()/sub | solution.py:73
  107.9 4.8 divide_convert_fusion
  116.7 3.4 reshape.336
  124.5 2.4 reshape.337
  130.3 4.2 fusion.40
  146.1 5.7 %collective-permute-start.5 = (bf16[2,6,6,192]{3,2,1,0:T(8,128)(2,1)S(1)}, bf16[2,6,6,192]{3,2,1,0:T(8,128)(2,1)S(1)}, u32[]{:S(2)}, u32[]{:S(2)}) collective-permute-start(bf16[2,6,6,192]{3,2,1,0:T(8,128)(2,1)S(1)} %get-tuple-element.38), channel_id=1, source_target_pairs={{1,0},{2,1},{3,2},{4,3},{5,4},{6,5},{7,6},{8,7},{9,8},{10,9},{11,1... | collective-permute-start | bytes 82952 | tf_op jit(solution)/shard_map/ppermute | solution.py:27
  153.5 2.9 collective-permute-start.6
  159.0 5.9 %collective-permute-done.7 = bf16[2,3,60,192]{3,2,1,0:T(8,128)(2,1)S(1)} collective-permute-done((bf16[2,3,60,192]{3,2,1,0:T(8,128)(2,1)S(1)}, bf16[2,3,60,192]{3,2,1,0:T(8,128)(2,1)S(1)}, u32[]{:S(2)}, u32[]{:S(2)}) %collective-permute-start.7) | collective-permute-done | bytes 138272 | tf_op jit(solution)/shard_map/ppermute | solution.py:27
  167.7 2.6 mul.449
  170.3 2.3 convolution_convert_fusion.22
  174.8 4.1 reshape.342
  178.8 5.7 %convolution_bitcast_fusion = f32[10,144,1,6,32]{1,4,3,0,2:T(8,128)} fusion(bf16[10,6,144,144]{2,3,1,0:T(8,128)(2,1)} %copy-done, bf16[10,6,32,144]{3,0,2,1:T(8,128)(2,1)} %bitcast.229), kind=kOutput, calls=%fused_computation.100 | convolution fusion | flops 79626240 | bytes 4147200 | tf_op jit(solution)/shard_map/transpose(jvp(nhqk,nkhd->nqhd))/dot_general | solution.py:75
  186.1 7.4 %fusion.6 = f32[10,6,144]{2,1,0:T(8,128)S(1)} fusion(f32[10,6,144,144]{2,3,1,0:T(8,128)} %get-tuple-element.53, bf16[10,6,144,144]{2,3,1,0:T(8,128)(2,1)S(1)} %convolution_convert_fusion.1, f32[10,6,144]{2,1,0:T(8,128)S(1)} %copy-done.67), kind=kLoop, calls=%fused_computation.8 | loop fusion | flops 4968000 | bytes 7534080 | tf_op jit(solution)/shard_map/transpose(jvp())/reduce_sum | solution.py:73
  193.6 6.4 %fusion.58 = f32[10,144,1,6,32]{1,4,3,0,2:T(8,128)} fusion(bf16[10,144,1,6,32]{1,0,4,3,2:T(8,128)(2,1)} %get-tuple-element.27, f32[10,6,144,144]{2,3,1,0:T(8,128)S(1)} %bitcast.219, bf16[10,6,144,144]{2,3,1,0:T(8,128)(2,1)} %copy-done.1, f32[10,6,144]{2,1,0:T(8,128)S(1)} %neg.45, f32[10,6,144]{2,1,0:T(8,128)S(1)} %copy-done.59, ...), kind=kOutput, calls=%fused_computation.99 | convolution fusion | flops 87091200 | bytes 9194400 | tf_op jit(solution)/shard_map/transpose(jvp(nqhd,nkhd->nhqk))/dot_general | solution.py:69
  200.0 6.5 %fusion.55 = f32[10,144,1,6,32]{1,4,3,0,2:T(8,128)} fusion(bf16[10,144,1,6,32]{1,0,4,3,2:T(8,128)(2,1)} %get-tuple-element.26, f32[10,6,144,144]{2,3,1,0:T(8,128)S(1)} %bitcast.219, bf16[10,6,144,144]{2,3,1,0:T(8,128)(2,1)} %copy-done.1, f32[10,6,144]{2,1,0:T(8,128)S(1)} %neg.45, f32[10,6,144]{2,1,0:T(8,128)S(1)} %copy-done.59, ...), kind=kOutput, calls=%fused_computation.98 | convolution fusion | flops 87091200 | bytes 9194400 | tf_op jit(solution)/shard_map/transpose(jvp(nqhd,nkhd->nhqk))/dot_general | solution.py:69
  206.5 5.1 fusion.162
  212.1 4.6 copy.170
  216.7 7.5 %convert_element_type.316 = bf16[1440,576]{0,1:T(8,128)(2,1)} reshape(bf16[10,144,3,6,32]{1,0,4,3,2:T(8,128)(2,1)} %copy.170) | data formatting | bytes 3317760 | tf_op jit(solution)/shard_map/transpose(jvp())/convert_element_type | solution.py:66
  224.2 3.4 convolution_convert_fusion.17
  258.9 2.3 convolution_bitcast_fusion.1
  286.4 7.8 %copy.186 = f32[2,192,2304]{1,0,2:T(2,128)} copy(f32[2,192,2304]{2,1,0:T(8,128)} %maximum_convert_fusion) | data formatting | bytes 7077888 | tf_op jit(solution)/shard_map/stack | solution.py:191
  296.8 155.2 %all-reduce.13.cloned.1.call-done = (f32[2,192,2304]{1,0,2:T(2,128)}, f32[2,124800]{1,0:T(2,128)}) async-done(((f32[2,192,2304]{1,0,2:T(2,128)}, f32[2,124800]{1,0:T(2,128)}), (f32[2,192,2304]{1,0,2:T(2,128)}, f32[2,124800]{1,0:T(2,128)})) %all-reduce.13.cloned.1.call-update) | async-done | bytes 4537360
  457.3 63.9 %psum.7 = f32[]{:T(128)} all-reduce(f32[]{:T(128)S(6)} %add.160), channel_id=1, replica_groups=mesh['lat'=4,'lon'=32] {'lat','lon'}, use_global_device_ids=true, to_apply=%region_32.33 | all-reduce | flops 1 | bytes 8 | tf_op jit(solution)/shard_map/psum | solution.py:203
  (386 shorter events, 146.2 us)
Async XLA Ops:
  7.2 6.1 %copy-start.42 = (bf16[2,192,576]{2,1,0:T(8,128)(2,1)S(1)}, bf16[2,192,576]{2,1,0:T(8,128)(2,1)}, u32[]{:S(2)}) copy-start(bf16[2,192,576]{2,1,0:T(8,128)(2,1)} %param.11) | copy-start | bytes 1327108
  7.2 444.8 %all-reduce.13.cloned.1.call-start = ((), (), s32[]{:S(2)}) async-start(), calls=%async_computation | async-start | bytes 11433984
  8.6 27.8 %copy-start.97 = (f32[1,1,192]{2,1,0:T(1,128)}, f32[1,1,192]{2,1,0:T(1,128)S(1)}, u32[]{:S(2)}) copy-start(f32[1,1,192]{2,1,0:T(1,128)S(1)} %get-tuple-element.42) | copy-start | bytes 2308
  36.0 6.3 %copy-start.2 = (f32[2,6,48,192]{3,2,1,0:T(8,128)}, f32[2,6,48,192]{3,2,1,0:T(8,128)S(1)}, u32[]{:S(2)}) copy-start(f32[2,6,48,192]{3,2,1,0:T(8,128)S(1)} %get-tuple-element.24) | copy-start | bytes 1327108
  42.3 10.8 %copy-start.64 = (f32[4,6,144]{2,1,0:T(8,128)S(1)}, f32[4,6,144]{2,1,0:T(8,128)}, u32[]{:S(2)}) copy-start(f32[4,6,144]{2,1,0:T(8,128)} %copy-done.63) | copy-start | bytes 41476
  44.7 15.4 %collective-permute-start = (bf16[2,6,6,192]{3,2,1,0:T(8,128)(2,1)}, bf16[2,6,6,192]{3,2,1,0:T(8,128)(2,1)}, u32[]{:S(2)}, u32[]{:S(2)}) collective-permute-start(bf16[2,6,6,192]{3,2,1,0:T(8,128)(2,1)} %get-tuple-element.39), channel_id=1, source_target_pairs={{0,1},{1,2},{2,3},{3,4},{4,5},{5,6},{6,7},{7,8},{8,9},{9,10},{10,1... | collective-permute-start | bytes 82952 | tf_op jit(solution)/shard_map/ppermute | solution.py:25
  46.8 13.3 %collective-permute-start.1 = (bf16[2,6,6,192]{3,2,1,0:T(8,128)(2,1)}, bf16[2,6,6,192]{3,2,1,0:T(8,128)(2,1)}, u32[]{:S(2)}, u32[]{:S(2)}) collective-permute-start(bf16[2,6,6,192]{3,2,1,0:T(8,128)(2,1)} %get-tuple-element.40), channel_id=1, source_target_pairs={{1,0},{2,1},{3,2},{4,3},{5,4},{6,5},{7,6},{8,7},{9,8},{10,9},{11,1... | collective-permute-start | bytes 82952 | tf_op jit(solution)/shard_map/ppermute | solution.py:27
  60.1 15.1 %copy-start.32 = (bf16[2,6,48,192]{3,2,1,0:T(8,128)(2,1)S(1)}, bf16[2,6,48,192]{3,2,1,0:T(8,128)(2,1)}, u32[]{:S(2)}) copy-start(bf16[2,6,48,192]{3,2,1,0:T(8,128)(2,1)} %copy-done.31) | copy-start | bytes 663556
  61.3 9.1 %collective-permute-start.2 = (bf16[2,3,60,192]{3,2,1,0:T(8,128)(2,1)S(1)}, bf16[2,3,60,192]{3,2,1,0:T(8,128)(2,1)S(1)}, u32[]{:S(2)}, u32[]{:S(2)}) collective-permute-start(bf16[2,3,60,192]{3,2,1,0:T(8,128)(2,1)S(1)} %get-tuple-element.35), channel_id=1, source_target_pairs={{0,32},{32,64},{64,96},{1,33},{33,65},{65,97},{2,34},{34,66},{66,9... | collective-permute-start | bytes 414728 | tf_op jit(solution)/shard_map/ppermute | solution.py:25
  66.7 8.5 %collective-permute-start.3 = (bf16[2,3,60,192]{3,2,1,0:T(8,128)(2,1)S(1)}, bf16[2,3,60,192]{3,2,1,0:T(8,128)(2,1)S(1)}, u32[]{:S(2)}, u32[]{:S(2)}) collective-permute-start(bf16[2,3,60,192]{3,2,1,0:T(8,128)(2,1)S(1)} %get-tuple-element.36), channel_id=1, source_target_pairs={{32,0},{64,32},{96,64},{33,1},{65,33},{97,65},{34,2},{66,34},{98,6... | collective-permute-start | bytes 414728 | tf_op jit(solution)/shard_map/ppermute | solution.py:27
  142.6 9.3 %copy-start.27 = (bf16[576,768]{1,0:T(8,128)(2,1)S(1)}, bf16[576,768]{1,0:T(8,128)(2,1)}, u32[]{:S(2)}) copy-start(bf16[576,768]{1,0:T(8,128)(2,1)} %copy-done.26) | copy-start | bytes 2654212
  142.6 9.2 %copy-start.57 = (bf16[2,6,48,192]{3,2,1,0:T(8,128)(2,1)S(1)}, bf16[2,6,48,192]{3,2,1,0:T(8,128)(2,1)}, u32[]{:S(2)}) copy-start(bf16[2,6,48,192]{3,2,1,0:T(8,128)(2,1)} %copy-done.56) | copy-start | bytes 663556
  146.0 18.9 %copy-start.19 = (bf16[2,6,48,192]{3,2,1,0:T(8,128)(2,1)}, bf16[2,6,48,192]{3,2,1,0:T(8,128)(2,1)S(1)}, u32[]{:S(2)}) copy-start(bf16[2,6,48,192]{3,2,1,0:T(8,128)(2,1)S(1)} %add_convert_fusion.5) | copy-start | bytes 663556
  146.0 12.3 %copy-start.58 = (f32[10,6,144]{2,1,0:T(8,128)S(1)}, f32[10,6,144]{2,1,0:T(8,128)}, u32[]{:S(2)}) copy-start(f32[10,6,144]{2,1,0:T(8,128)} %get-tuple-element.52) | copy-start | bytes 103684
  146.1 7.2 %collective-permute-start.4 = (bf16[2,6,6,192]{3,2,1,0:T(8,128)(2,1)S(1)}, bf16[2,6,6,192]{3,2,1,0:T(8,128)(2,1)S(1)}, u32[]{:S(2)}, u32[]{:S(2)}) collective-permute-start(bf16[2,6,6,192]{3,2,1,0:T(8,128)(2,1)S(1)} %get-tuple-element.37), channel_id=1, source_target_pairs={{0,1},{1,2},{2,3},{3,4},{4,5},{5,6},{6,7},{7,8},{8,9},{9,10},{10,1... | collective-permute-start | bytes 82952 | tf_op jit(solution)/shard_map/ppermute | solution.py:25
  146.1 7.1 %collective-permute-start.5 = (bf16[2,6,6,192]{3,2,1,0:T(8,128)(2,1)S(1)}, bf16[2,6,6,192]{3,2,1,0:T(8,128)(2,1)S(1)}, u32[]{:S(2)}, u32[]{:S(2)}) collective-permute-start(bf16[2,6,6,192]{3,2,1,0:T(8,128)(2,1)S(1)} %get-tuple-element.38), channel_id=1, source_target_pairs={{1,0},{2,1},{3,2},{4,3},{5,4},{6,5},{7,6},{8,7},{9,8},{10,9},{11,1... | collective-permute-start | bytes 82952 | tf_op jit(solution)/shard_map/ppermute | solution.py:27
  153.5 12.4 %copy-start.107 = (bf16[2,5]{1,0:T(2,128)(2,1)S(1)}, bf16[2,5]{1,0:T(2,128)(2,1)}, u32[]{:S(2)}) copy-start(bf16[2,5]{1,0:T(2,128)(2,1)} %fusion.144) | copy-start | bytes 64
  153.5 5.5 %collective-permute-start.6 = (bf16[2,3,60,192]{3,2,1,0:T(8,128)(2,1)S(1)}, bf16[2,3,60,192]{3,2,1,0:T(8,128)(2,1)S(1)}, u32[]{:S(2)}, u32[]{:S(2)}) collective-permute-start(bf16[2,3,60,192]{3,2,1,0:T(8,128)(2,1)S(1)} %get-tuple-element.33), channel_id=1, source_target_pairs={{0,32},{32,64},{64,96},{1,33},{33,65},{65,97},{2,34},{34,66},{66,9... | collective-permute-start | bytes 414728 | tf_op jit(solution)/shard_map/ppermute | solution.py:25
  156.4 8.5 %collective-permute-start.7 = (bf16[2,3,60,192]{3,2,1,0:T(8,128)(2,1)S(1)}, bf16[2,3,60,192]{3,2,1,0:T(8,128)(2,1)S(1)}, u32[]{:S(2)}, u32[]{:S(2)}) collective-permute-start(bf16[2,3,60,192]{3,2,1,0:T(8,128)(2,1)S(1)} %get-tuple-element.34), channel_id=1, source_target_pairs={{32,0},{64,32},{96,64},{33,1},{65,33},{97,65},{34,2},{66,34},{98,6... | collective-permute-start | bytes 414728 | tf_op jit(solution)/shard_map/ppermute | solution.py:27
  178.8 5.7 %copy-start.16 = (bf16[10,144,6,32]{1,0,3,2:T(8,128)(2,1)S(1)}, bf16[10,144,6,32]{1,0,3,2:T(8,128)(2,1)}, u32[]{:S(2)}) copy-start(bf16[10,144,6,32]{1,0,3,2:T(8,128)(2,1)} %reshape.342) | copy-start | bytes 1658884
  178.8 14.7 %slice-start = ((s8[8847360]{0:T(1024)(128)(4,1)}), s8[4194304]{0:T(1024)(128)(4,1)S(1)}, s32[]{:S(2)}) async-start(s8[8847360]{0:T(1024)(128)(4,1)} %bitcast.218), calls=%async_computation.1 | async-start | bytes 8388608
  184.5 9.0 %slice-start.1 = ((s8[8847360]{0:T(1024)(128)(4,1)}), s8[4194304]{0:T(1024)(128)(4,1)S(1)}, s32[]{:S(2)}) async-start(s8[8847360]{0:T(1024)(128)(4,1)} %bitcast.218), calls=%async_computation.2 | async-start | bytes 8388608
  186.1 7.4 %copy-start.1 = (bf16[10,6,144,144]{2,3,1,0:T(8,128)(2,1)}, bf16[10,6,144,144]{2,3,1,0:T(8,128)(2,1)S(1)}, u32[]{:S(2)}) copy-start(bf16[10,6,144,144]{2,3,1,0:T(8,128)(2,1)S(1)} %convolution_convert_fusion.1) | copy-start | bytes 7464964
  186.1 7.5 %slice-start.2 = ((s8[8847360]{0:T(1024)(128)(4,1)}), s8[458752]{0:T(1024)(128)(4,1)S(1)}, s32[]{:S(2)}) async-start(s8[8847360]{0:T(1024)(128)(4,1)} %bitcast.218), calls=%async_computation.3 | async-start | bytes 917504
  186.1 7.5 %copy-start.59 = (f32[10,6,144]{2,1,0:T(8,128)S(1)}, f32[10,6,144]{2,1,0:T(8,128)}, u32[]{:S(2)}) copy-start(f32[10,6,144]{2,1,0:T(8,128)} %get-tuple-element.52) | copy-start | bytes 103684
  186.1 7.5 %copy-start.103 = (pred[10,144]{1,0:T(8,128)(4,1)S(1)}, pred[10,144]{1,0:T(8,128)(4,1)}, u32[]{:S(2)}) copy-start(pred[10,144]{1,0:T(8,128)(4,1)} %transpose.117) | copy-start | bytes 4324
  240.9 5.7 %copy-start.79 = (f32[2,6,48]{2,1,0:T(8,128)S(1)}, f32[2,6,48]{2,1,0:T(8,128)}, u32[]{:S(2)}) copy-start(f32[2,6,48]{2,1,0:T(8,128)} %copy-done.78) | copy-start | bytes 6916
  286.4 7.8 %copy-start.39 = (f32[1,124800]{1,0:T(1,128)S(1)}, f32[1,124800]{1,0:T(1,128)}, u32[]{:S(2)}) copy-start(f32[1,124800]{1,0:T(1,128)} %stack.27) | copy-start | bytes 1497604
  296.1 160.0 %copy-start.36 = (bf16[2,6,48,192]{3,2,1,0:T(8,128)(2,1)S(1)}, bf16[2,6,48,192]{3,2,1,0:T(8,128)(2,1)}, u32[]{:S(2)}) copy-start(bf16[2,6,48,192]{3,2,1,0:T(8,128)(2,1)} %copy-done.35) | copy-start | bytes 663556
  296.1 160.0 %copy-start.77 = (f32[2,6,48]{2,1,0:T(8,128)S(1)}, f32[2,6,48]{2,1,0:T(8,128)}, u32[]{:S(2)}) copy-start(f32[2,6,48]{2,1,0:T(8,128)} %copy-done.75) | copy-start | bytes 6916
  296.1 160.1 %copy-start.86 = (f32[2,6,48]{2,1,0:T(8,128)S(1)}, f32[2,6,48]{2,1,0:T(8,128)}, u32[]{:S(2)}) copy-start(f32[2,6,48]{2,1,0:T(8,128)} %copy-done.85) | copy-start | bytes 6916
  296.1 160.1 %copy-start.96 = (f32[1,1,192]{2,1,0:T(1,128)S(1)}, f32[1,1,192]{2,1,0:T(1,128)}, u32[]{:S(2)}) copy-start(f32[1,1,192]{2,1,0:T(1,128)} %copy-done.94) | copy-start | bytes 2308
  (91 other events, 219.3 us)
Sparse Core Ops, SparseCore 0:
  296.3 155.7 all-reduce.12
where the time goes:
time: 542 us; the launch traced here: 532 us
  waiting for transfers between devices  166 us (31%)
  local copies, waits for them, and re-layouts  117 us (22%)
  matrix products  80.1 us (15%)
  blocking collectives  63.9 us (12%)
  other arithmetic  60.8 us (11%)
  starting transfers between devices  26.2 us (5%)
  between operations  18 us (3%)
    unnamed x2, waiting for transfers between devices  155 us
    psum x1, blocking collectives, shards(): lax.psum(jnp.sum(matrix * matrix) + jnp.sum(remainder * remainder), ('lat...  63.9 us
    ppermute x4, starting transfers between devices, padded(): lax.ppermute(head, axis, [((i + 1) % count, i) for i in range(ends)])  15.7 us
    dot_general x5, matrix products, window_attention(): jnp.einsum('nqhd,nkhd->nhqk', packed[:, :, 0], packed[:, :, 1])  15.3 us
    dot_general x6, matrix products, feed_forward(): jnp.dot(normed, w_up, preferred_element_type=jnp.float32)  14.4 us
    convert_element_type x4, local copies, waits for them, and re-layouts, window_attention(): lax.optimization_barrier(packed.astype(jnp.bfloat16)).astype(jnp.float32)  14 us
    dot_general x6, matrix products, window_attention(): jnp.dot(mixed_heads.reshape(window_count * tokens_win, channels), w_proj,...  12.7 us
    dot_general x6, matrix products, window_attention(): jnp.einsum('nhqk,nkhd->nqhd', weights, packed[:, :, 2]).astype(jnp.bfloat16)  11.4 us
  transfers between devices with their start and end apart: 9, of which 4 were waited for; matrix products, arithmetic and copies ran while one was open for 2% of the time, Pallas kernels for 0%

commit v1 on v0

v1 whole, which is shorter than its diff:
```python
import functools
import math

import jax
import jax.numpy as jnp
import numpy as np
from jax import lax
from jax.experimental import pallas as pl
from jax.experimental.pallas import tpu as pltpu
from jax.sharding import PartitionSpec as P

C = 192
HEADS = 6
HEAD = 32
FFN = 768
WT = 144
NT = 576
NR = 640
QT = 160
MAIN = 112
VECB = 124800
BROWS = HEADS * WT
MROWS = 2304
OROWS = 880
GROWS = MROWS + OROWS
LOG2E = math.log2(math.e)
MESH = pl.DeviceIdType.MESH
BF = jnp.bfloat16
F32 = jnp.float32
VMEM_LIMIT = 56 * 1024 * 1024


def nat(l, r, c):
    return l * 288 + r * 48 + c


def one_hot(sources, width):
    mat = np.zeros((len(sources), width), np.float32)
    for i, s in enumerate(sources):
        if s >= 0:
            mat[i, s] = 1.0
    return mat


@functools.cache
def orders():
    win = [nat(l, r, 12 * w + c) for w in range(4) for l in range(2) for r in range(6) for c in range(12)]

    def cells(rows, cols, size):
        out = [nat(l, r, c) for l in range(2) for r in rows for c in cols]
        return out + [-1] * (size - len(out))

    top, low = range(0, 3), range(3, 6)
    send = []
    for rows in (top, low):
        send += cells(rows, range(0, 18), MAIN)
        send += cells(rows, range(42, 48), QT - MAIN)
        send += cells(rows, range(24, 42), MAIN)
        send += cells(rows, range(18, 24), QT - MAIN)
    slots = []
    for s in range(4):
        for l in range(2):
            for half in range(2):
                for r in range(3):
                    for cc in range(12):
                        col = 12 * (s % 2) + cc
                        base = QT * (2 * (s // 2) + half)
                        if col >= 6:
                            slots.append(base + (l * 3 + r) * 18 + col - 6)
                        else:
                            slots.append(base + MAIN + (l * 3 + r) * 6 + col)
    win_at = {n: i for i, n in enumerate(win)}
    send_win = [win_at[n] if n >= 0 else -1 for n in send]
    to_win = one_hot(win, NT)
    send_from_win = one_hot(send_win, NT)
    send_from_nat = one_hot(send, NT)
    to_slots = one_hot(slots, NR)
    return {
        "to_win": to_win,
        "to_nat": to_win.T.copy(),
        "send_win": send_from_win,
        "win_send": send_from_win.T.copy(),
        "send_nat": send_from_nat,
        "to_slots": to_slots,
        "from_slots": to_slots.T.copy(),
    }


def const(name):
    return jnp.asarray(orders()[name], BF)


def nn(a, b):
    return lax.dot_general(a, b, (((1,), (0,)), ((), ())), preferred_element_type=F32)


def nt(a, b):
    return lax.dot_general(a, b, (((1,), (1,)), ((), ())), preferred_element_type=F32)


def tn(a, b):
    return lax.dot_general(a, b, (((0,), (0,)), ((), ())), preferred_element_type=F32)


def shuffle(mat, x):
    return nn(mat, x).astype(BF)


def stats(x):
    center = x - jnp.mean(x, axis=-1, keepdims=True)
    r = lax.rsqrt(jnp.mean(center * center, axis=-1, keepdims=True) + 1e-05)
    return center * r, r


def norm_back(dn, gain, xhat, r):
    t = dn * gain
    return r * (t - jnp.mean(t, axis=-1, keepdims=True) - xhat * jnp.mean(t * xhat, axis=-1, keepdims=True))


def head_mask(h, dtype):
    lane = lax.broadcasted_iota(jnp.int32, (1, C), 1)
    return ((lane >= h * HEAD) & (lane < (h + 1) * HEAD)).astype(F32).astype(dtype)


def forward_windows(x_ref, gains, wq_ref, wproj_ref, wup_ref, wdown_ref, bias_of, q_ref, k_ref, v_ref, p_ref, mix_ref, hid_ref, a_ref, gp_ref, out_ref):
    g0, g1 = gains

    def window(w, carry):
        rows = pl.ds(pl.multiple_of(w * WT, WT), WT)
        x = x_ref[rows, :].astype(F32)
        u = (stats(x)[0] * g0).astype(BF)
        q = nn(u, wq_ref[0]).astype(BF)
        k = nn(u, wq_ref[1]).astype(BF)
        v = nn(u, wq_ref[2]).astype(BF)
        q_ref[rows, :] = q
        k_ref[rows, :] = k
        v_ref[rows, :] = v
        mixed = jnp.zeros((WT, C), F32)
        for h in range(HEADS):
            s = nt(q * head_mask(h, BF), k) * (HEAD ** -0.5 * LOG2E) + bias_of(w, h)
            e = jnp.exp2(s - jnp.max(s, axis=-1, keepdims=True))
            p = (e * (1.0 / jnp.sum(e, axis=-1, keepdims=True))).astype(BF)
            p_ref[pl.ds(pl.multiple_of(w * BROWS + h * WT, WT), WT), :] = p
            mixed = mixed + nn(p, v) * head_mask(h, F32)
        mixed = mixed.astype(BF)
        mix_ref[rows, :] = mixed
        attended = nn(mixed, wproj_ref[...]).astype(BF)
        hidden = x + attended.astype(F32)
        hid_ref[rows, :] = hidden
        n2 = (stats(hidden)[0] * g1).astype(BF)
        total = hidden
        for j in range(3):
            cols = slice(256 * j, 256 * j + 256)
            up = nn(n2, wup_ref[:, cols])
            cdf = 0.5 + 0.5 * lax.erf(up * (0.5 ** 0.5))
            slope = cdf + up * jnp.exp2(up * up * (-0.5 * LOG2E)) * (1.0 / math.sqrt(2 * math.pi))
            act = (up * cdf).astype(BF)
            a_ref[rows, cols] = act
            gp_ref[rows, cols] = slope.astype(BF)
            if out_ref is not None:
                total = total + nn(act, wdown_ref[cols, :])
        if out_ref is not None:
            out_ref[rows, :] = total.astype(BF)
        return carry

    lax.fori_loop(0, 4, window, 0)


def backward_windows(dout_ref, x_ref, gains, wq_ref, wproj_ref, wup_ref, wdown_ref, q_ref, k_ref, v_ref, p_ref, mix_ref, hid_ref, a_ref, gp_ref,
                     dbias_of, dg_ref, dup_ref, n2_ref, datt_ref, dq_ref, dk_ref, dv_ref, u_ref, dom_ref, qm_ref, ds_ref, dx_ref):
    g0, g1 = gains
    dg_ref[...] = jnp.zeros((2, C), F32)

    def window(w, carry):
        rows = pl.ds(pl.multiple_of(w * WT, WT), WT)
        dy = dout_ref[rows, :]
        dn2 = jnp.zeros((WT, C), F32)
        for j in range(3):
            cols = slice(256 * j, 256 * j + 256)
            da = nt(dy, wdown_ref[cols, :]).astype(BF).astype(F32)
            dup = (da * gp_ref[rows, cols].astype(F32)).astype(BF)
            dup_ref[rows, cols] = dup
            dn2 = dn2 + nt(dup, wup_ref[:, cols])
        dn2 = dn2.astype(BF).astype(F32)
        xhat, r = stats(hid_ref[rows, :])
        n2_ref[rows, :] = (xhat * g1).astype(BF)
        dg_ref[1:2, :] += jnp.sum(dn2 * xhat, axis=0, keepdims=True)
        dhid = dy.astype(F32) + norm_back(dn2, g1, xhat, r)
        datt = dhid.astype(BF)
        datt_ref[rows, :] = datt
        dmix = nt(datt, wproj_ref[...]).astype(BF)
        q = q_ref[rows, :]
        k = k_ref[rows, :]
        v = v_ref[rows, :]
        dq = jnp.zeros((WT, C), F32)
        for h in range(HEADS):
            part = slice(h * WT, h * WT + WT)
            prow = pl.ds(pl.multiple_of(w * BROWS + h * WT, WT), WT)
            dom = dmix * head_mask(h, BF)
            dom_ref[part, :] = dom
            qm_ref[part, :] = q * head_mask(h, BF)
            dp = nt(dom, v)
            p = p_ref[prow, :].astype(F32)
            t = p * dp
            ds = t - p * jnp.sum(t, axis=-1, keepdims=True)
            dbias_of(w, h, ds)
            dsb = ds.astype(BF)
            ds_ref[part, :] = dsb
            dq = dq + nn(dsb, k) * head_mask(h, F32)
        pw = p_ref[pl.ds(pl.multiple_of(w * BROWS, WT), BROWS), :]
        dq = (dq * HEAD ** -0.5).astype(BF)
        dk = (tn(ds_ref[...], qm_ref[...]) * HEAD ** -0.5).astype(BF)
        dv = tn(pw, dom_ref[...]).astype(BF)
        dq_ref[rows, :] = dq
        dk_ref[rows, :] = dk
        dv_ref[rows, :] = dv
        du = nt(dq, wq_ref[0]) + nt(dk, wq_ref[1]) + nt(dv, wq_ref[2])
        du = du.astype(BF).astype(F32)
        xhat, r = stats(x_ref[rows, :].astype(F32))
        u_ref[rows, :] = (xhat * g0).astype(BF)
        dg_ref[0:1, :] += jnp.sum(du * xhat, axis=0, keepdims=True)
        dx = norm_back(du, g0, xhat, r).astype(BF).astype(F32) + datt.astype(F32)
        dx_ref[rows, :] = dx.astype(BF)
        return carry

    lax.fori_loop(0, 4, window, 0)


def split_qkv(wqkv_ref, wq_ref):
    for i in range(3):
        wq_ref[i] = wqkv_ref[:, C * i:C * i + C]


def weight_products(emit, u, n2, mix, dout, dq_ref, dk_ref, dv_ref, datt_ref, dup_ref, a_ref):
    emit(0, tn(dq_ref[...], u))
    emit(192, tn(dk_ref[...], u))
    emit(384, tn(dv_ref[...], u))
    emit(576, tn(datt_ref[...], mix))
    for j in range(3):
        cols = slice(256 * j, 256 * j + 256)
        emit(768 + 256 * j, tn(dup_ref[:, cols], n2))
    for j in range(3):
        cols = slice(256 * j, 256 * j + 256)
        emit(1536 + 256 * j, tn(a_ref[:, cols], dout))


def first_forward(tok_ref, cot_ref, gains_ref, wqkv_ref, wproj_ref, wup_ref, wdown_ref, bias_ref, to_win_ref, send_win_ref, send_nat_ref,
                  x_ref, q_ref, k_ref, v_ref, p_ref, mix_ref, hid_ref, a_ref, gp_ref, send_ref, wq_ref, lbias_ref, out_ref):
    x_ref[...] = shuffle(to_win_ref[...], tok_ref[...])
    split_qkv(wqkv_ref, wq_ref)
    lbias_ref[...] = bias_ref[...] * LOG2E
    gains = (gains_ref[0:1, :], gains_ref[1:2, :])

    def bias_of(w, h):
        return lbias_ref[h * WT:h * WT + WT, :]

    forward_windows(x_ref, gains, wq_ref, wproj_ref, wup_ref, wdown_ref, bias_of, q_ref, k_ref, v_ref, p_ref, mix_ref, hid_ref, a_ref, gp_ref, out_ref)
    send_ref[:, 0:C] = shuffle(send_win_ref[...], out_ref[...])
    send_ref[:, C:2 * C] = shuffle(send_nat_ref[...], cot_ref[...])


def whole(shape):
    return pl.BlockSpec(shape, lambda i: (0,) * len(shape))


def block_of(shape, b):
    return pl.BlockSpec((pl.squeezed,) + shape, lambda i: (b,) + (0,) * len(shape))


def params(**kw):
    return pltpu.CompilerParams(vmem_limit_bytes=VMEM_LIMIT, **kw)


def weight_specs(b):
    return [block_of((2, C), b), block_of((C, 3 * C), b), block_of((C, C), b), block_of((C, FFN), b), block_of((FFN, C), b), block_of((BROWS, WT), b)]


RESIDUALS = [((NT, C), BF), ((NT, C), BF), ((NT, C), BF), ((NT, C), BF), ((4 * BROWS, WT), BF), ((NT, C), BF), ((NT, C), F32), ((NT, FFN), BF), ((NT, FFN), BF)]


def run_first_forward(tok, cot, weights):
    perms = [const("to_win"), const("send_win"), const("send_nat")]
    outs = RESIDUALS + [((NR, 2 * C), BF)]
    return pl.pallas_call(
        first_forward,
        grid=(1,),
        in_specs=[whole((NT, C)), whole((NT, C))] + weight_specs(0) + [whole(p.shape) for p in perms],
        out_specs=[whole(s) for s, _ in outs],
        out_shape=[jax.ShapeDtypeStruct(s, d) for s, d in outs],
        scratch_shapes=[pltpu.VMEM((3, C, C), BF), pltpu.VMEM((BROWS, WT), F32), pltpu.VMEM((NT, C), BF)],
        compiler_params=params(),
        name="first_forward",
    )(tok, cot, *weights, *perms)


BACK_SCRATCH = [
    pltpu.VMEM((2, C), F32), pltpu.VMEM((NT, FFN), BF), pltpu.VMEM((NT, C), BF), pltpu.VMEM((NT, C), BF),
    pltpu.VMEM((NT, C), BF), pltpu.VMEM((NT, C), BF), pltpu.VMEM((NT, C), BF), pltpu.VMEM((NT, C), BF),
    pltpu.VMEM((BROWS, C), BF), pltpu.VMEM((BROWS, C), BF), pltpu.VMEM((BROWS, WT), BF), pltpu.VMEM((NT, C), BF),
]


def half_of(shape, axis):
    return (lax.broadcasted_iota(jnp.int32, shape, axis) // 36) % 2


def lane_moves(low):
    src = lax.broadcasted_iota(jnp.int32, (WT, WT), 0)
    dst = lax.broadcasted_iota(jnp.int32, (WT, WT), 1)
    keep = dst - 36 * ((dst // 36) % 2) + (0 if low else 36)
    return (src == keep).astype(F32)


def polar_bias(table, low):
    moved = jnp.dot(table, lane_moves(low), precision=lax.Precision.HIGHEST, preferred_element_type=F32)
    half = half_of((WT, WT), 0)
    if low:
        moved = jnp.where(half == 0, moved, pltpu.roll(moved, 36, 0))
    else:
        moved = jnp.where(half == 1, moved, pltpu.roll(moved, WT - 36, 0))
    return jnp.where(half == half_of((WT, WT), 1), moved, -1e30)


def polar_back(grad, low):
    half = half_of((WT, WT), 0)
    if low:
        folded = jnp.where(half == 0, grad + pltpu.roll(grad, WT - 36, 0), 0.0)
    else:
        folded = jnp.where(half == 1, grad + pltpu.roll(grad, 36, 0), 0.0)
    return lax.dot_general(folded, lane_moves(low), (((1,), (1,)), ((), ())), precision=lax.Precision.HIGHEST, preferred_element_type=F32)


def second_block(band_ref, recv_ref, gains_ref, wqkv_ref, wproj_ref, wup_ref, wdown_ref, bias_ref, to_slots_ref, from_slots_ref,
                 back_ref, grad_ref, dbias_ref, dg_ref,
                 wq_ref, lbias_ref, q_ref, k_ref, v_ref, p_ref, mix_ref, hid_ref, a_ref, gp_ref, x_ref, cot_ref,
                 dgs_ref, dup_ref, n2_ref, datt_ref, dq_ref, dk_ref, dv_ref, u_ref, dom_ref, qm_ref, ds_ref, dx_ref, dbs_ref):
    x_ref[...] = shuffle(to_slots_ref[...], recv_ref[:, 0:C])
    cot_ref[...] = shuffle(to_slots_ref[...], recv_ref[:, C:2 * C])
    split_qkv(wqkv_ref, wq_ref)
    band = band_ref[0]
    gains = (gains_ref[0:1, :], gains_ref[1:2, :])
    for group in range(2):
        polar = band == (0 if group == 0 else 3)

        @pl.when(polar)
        def _():
            for h in range(HEADS):
                rows = slice(h * WT, h * WT + WT)
                lbias_ref[group, rows, :] = polar_bias(bias_ref[rows, :] * LOG2E, group == 1)

        @pl.when(jnp.logical_not(polar))
        def _():
            lbias_ref[group] = bias_ref[...] * LOG2E

    dbs_ref[...] = jnp.zeros((2, BROWS, WT), F32)

    def bias_of(w, h):
        return lbias_ref[w // 2, h * WT:h * WT + WT, :]

    def dbias_of(w, h, ds):
        dbs_ref[w // 2, h * WT:h * WT + WT, :] += ds

    forward_windows(x_ref, gains, wq_ref, wproj_ref, wup_ref, wdown_ref, bias_of, q_ref, k_ref, v_ref, p_ref, mix_ref, hid_ref, a_ref, gp_ref, None)
    backward_windows(cot_ref, x_ref, gains, wq_ref, wproj_ref, wup_ref, wdown_ref, q_ref, k_ref, v_ref, p_ref, mix_ref, hid_ref, a_ref, gp_ref,
                     dbias_of, dgs_ref, dup_ref, n2_ref, datt_ref, dq_ref, dk_ref, dv_ref, u_ref, dom_ref, qm_ref, ds_ref, dx_ref)
    back_ref[...] = shuffle(from_slots_ref[...], dx_ref[...])
    dg_ref[...] = dgs_ref[...]
    for group in range(2):
        polar = band == (0 if group == 0 else 3)

        @pl.when(polar)
        def _():
            for h in range(HEADS):
                rows = slice(h * WT, h * WT + WT)
                dbs_ref[group, rows, :] = polar_back(dbs_ref[group, rows, :], group == 1)

    dbias_ref[...] = dbs_ref[0] + dbs_ref[1]

    def shifted(ref):
        return jnp.concatenate([jnp.zeros((NT, 64), BF), ref[...]], axis=1)

    def emit(row, value):
        grad_ref[row:row + value.shape[0], :] = value.astype(BF)

    weight_products(emit, shifted(u_ref), shifted(n2_ref), shifted(mix_ref), shifted(cot_ref), dq_ref, dk_ref, dv_ref, datt_ref, dup_ref, a_ref)


def run_second_block(band, recv, weights):
    perms = [const("to_slots"), const("from_slots")]
    outs = [((NR, C), BF), ((MROWS, 256), BF), ((BROWS, WT), F32), ((2, C), F32)]
    fwd_scratch = [pltpu.VMEM(s, d) for s, d in RESIDUALS[1:]]
    return pl.pallas_call(
        second_block,
        grid=(1,),
        in_specs=[pl.BlockSpec(memory_space=pltpu.SMEM), whole((NR, 2 * C))] + weight_specs(1) + [whole(p.shape) for p in perms],
        out_specs=[whole(s) for s, _ in outs],
        out_shape=[jax.ShapeDtypeStruct(s, d) for s, d in outs],
        scratch_shapes=[pltpu.VMEM((3, C, C), BF), pltpu.VMEM((2, BROWS, WT), F32)] + fwd_scratch
        + [pltpu.VMEM((NT, C), BF), pltpu.VMEM((NT, C), BF)] + BACK_SCRATCH + [pltpu.VMEM((2, BROWS, WT), F32)],
        compiler_params=params(),
        name="second_block",
    )(band, recv, *weights, *perms)


def first_backward(ret_ref, gains_ref, wqkv_ref, wproj_ref, wup_ref, wdown_ref, bias_ref, x_ref, q_ref, k_ref, v_ref, p_ref, mix_ref, hid_ref,
                   a_ref, gp_ref, grad2_ref, dbias2_ref, dg2_ref, win_send_ref, to_nat_ref,
                   gtok_ref, grad_ref,
                   wq_ref, dout_ref, dg_ref, dup_ref, n2_ref, datt_ref, dq_ref, dk_ref, dv_ref, u_ref, dom_ref, qm_ref, ds_ref, dx_ref, dbs_ref):
    dout_ref[...] = shuffle(win_send_ref[...], ret_ref[...])
    split_qkv(wqkv_ref, wq_ref)
    gains = (gains_ref[0:1, :], gains_ref[1:2, :])
    dbs_ref[...] = jnp.zeros((BROWS, WT), F32)

    def dbias_of(w, h, ds):
        dbs_ref[h * WT:h * WT + WT, :] += ds

    backward_windows(dout_ref, x_ref, gains, wq_ref, wproj_ref, wup_ref, wdown_ref, q_ref, k_ref, v_ref, p_ref, mix_ref, hid_ref, a_ref, gp_ref,
                     dbias_of, dg_ref, dup_ref, n2_ref, datt_ref, dq_ref, dk_ref, dv_ref, u_ref, dom_ref, qm_ref, ds_ref, dx_ref)
    gtok_ref[...] = shuffle(to_nat_ref[...], dx_ref[...])

    def widened(ref):
        return jnp.concatenate([ref[...], jnp.zeros((NT, 64), BF)], axis=1)

    def emit(row, value):
        rows = slice(row, row + value.shape[0])
        other = grad2_ref[rows, :]
        grad_ref[rows, 0:128] = value[:, 0:128].astype(BF)
        grad_ref[rows, 128:256] = (value[:, 128:256] + other[:, 0:128].astype(F32)).astype(BF)
        grad_ref[rows, 256:384] = other[:, 128:256]

    weight_products(emit, widened(u_ref), widened(n2_ref), widened(mix_ref), widened(dout_ref), dq_ref, dk_ref, dv_ref, datt_ref, dup_ref, a_ref)
    pad = jnp.zeros((BROWS, 384 - 2 * WT), F32)
    grad_ref[MROWS:MROWS + BROWS, :] = jnp.concatenate([dbs_ref[...], dbias2_ref[...], pad], axis=1).astype(BF)

    def gain_rows(ref):
        flat = jnp.concatenate([ref[0:1, :], ref[1:2, :], jnp.zeros((1, 3 * WT - 2 * C), F32)], axis=1)
        return jnp.concatenate([flat[:, 0:WT], flat[:, WT:2 * WT], flat[:, 2 * WT:3 * WT]], axis=0)

    gains_out = jnp.concatenate([gain_rows(dg_ref), gain_rows(dg2_ref), jnp.zeros((3, 384 - 2 * WT), F32)], axis=1)
    grad_ref[MROWS + BROWS:GROWS, :] = jnp.concatenate([gains_out, jnp.zeros((GROWS - MROWS - BROWS - 3, 384), F32)], axis=0).astype(BF)


def run_first_backward(ret, weights, residuals, grad2, dbias2, dg2):
    perms = [const("win_send"), const("to_nat")]
    outs = [((NT, C), BF), ((GROWS, 384), BF)]
    extra = [grad2, dbias2, dg2]
    return pl.pallas_call(
        first_backward,
        grid=(1,),
        in_specs=[whole((NR, C))] + weight_specs(0) + [whole(s) for s, _ in RESIDUALS] + [whole(e.shape) for e in extra] + [whole(p.shape) for p in perms],
        out_specs=[whole(s) for s, _ in outs],
        out_shape=[jax.ShapeDtypeStruct(s, d) for s, d in outs],
        scratch_shapes=[pltpu.VMEM((3, C, C), BF), pltpu.VMEM((NT, C), BF)] + BACK_SCRATCH + [pltpu.VMEM((BROWS, WT), F32)],
        compiler_params=params(),
        name="first_backward",
    )(ret, *weights, *residuals, *extra, *perms)


def greet(peers, count):
    barrier = pltpu.get_barrier_semaphore()
    for cond, dev in peers:
        if cond is None:
            pl.semaphore_signal(barrier, inc=1, device_id=dev, device_id_type=MESH)
        else:
            @pl.when(cond)
            def _():
                pl.semaphore_signal(barrier, inc=1, device_id=dev, device_id_type=MESH)
    pl.semaphore_wait(barrier, count)


def exchange(moves_of, nlat, nlon, src, dst, send_sem, recv_sem, local_sem):
    b = lax.axis_index("lat")
    j = lax.axis_index("lon")
    east, west = lax.rem(j + 1, nlon), lax.rem(j + nlon - 1, nlon)
    up, down = jnp.maximum(b - 1, 0), jnp.minimum(b + 1, nlat - 1)
    first, last = b == 0, b == nlat - 1
    inner_up, inner_down = b > 0, b < nlat - 1
    greet([(None, (b, east)), (None, (b, west)), (inner_up, (up, j)), (inner_down, (down, j)), (inner_up, (up, east)), (inner_down, (down, west))], jnp.where(jnp.logical_or(first, last), 4, 6))
    sends, locals_, recvs = moves_of(b, j, east, west, up, down, first, last, inner_up, inner_down)

    def remote(i, s, d, size, dev):
        return pltpu.make_async_remote_copy(src_ref=src.at[pl.ds(s, size), :], dst_ref=dst.at[pl.ds(d, size), :], send_sem=send_sem.at[i], recv_sem=recv_sem.at[i], device_id=dev, device_id_type=MESH)

    def local(i, s, d, size):
        return pltpu.make_async_copy(src.at[pl.ds(s, size), :], dst.at[pl.ds(d, size), :], local_sem.at[i])

    def guarded(cond, act):
        if cond is None:
            act()
        else:
            pl.when(cond)(act)

    for i, cond, s, d, size, dev in sends:
        guarded(cond, lambda: remote(i, s, d, size, dev).start())
    for i, (cond, s, d, size) in enumerate(locals_):
        guarded(cond, lambda: local(i, s, d, size).start())
    for i, cond, d, size in recvs:
        guarded(cond, lambda: remote(i, 0, d, size, (b, east)).wait_recv())
    for i, (cond, s, d, size) in enumerate(locals_):
        guarded(cond, lambda: local(i, s, d, size).wait())
    for i, cond, s, d, size, dev in sends:
        guarded(cond, lambda: remote(i, s, d, size, dev).wait_send())


def moves_out(b, j, east, west, up, down, first, last, inner_up, inner_down):
    sends = [
        (0, None, 432, 432, 48, (b, east)),
        (1, inner_up, 112, 592, 48, (up, east)),
        (2, first, 112, 112, 48, (b, east)),
        (3, inner_up, 0, 480, 112, (up, j)),
        (4, inner_down, 480, 0, 160, (down, j)),
    ]
    locals_ = [(None, 160, 160, 272), (first, 0, 0, 112), (last, 480, 480, 160)]
    recvs = [(0, None, 432, 48), (1, inner_down, 592, 48), (2, first, 112, 48), (3, inner_down, 480, 112), (4, inner_up, 0, 160)]
    return sends, locals_, recvs


def moves_back(b, j, east, west, up, down, first, last, inner_up, inner_down):
    sends = [
        (0, None, 432, 432, 48, (b, west)),
        (1, inner_down, 592, 112, 48, (down, west)),
        (2, first, 112, 112, 48, (b, west)),
        (3, inner_down, 480, 0, 112, (down, j)),
        (4, inner_up, 0, 480, 160, (up, j)),
    ]
    locals_ = [(None, 160, 160, 272), (first, 0, 0, 112), (last, 480, 480, 160)]
    recvs = [(0, None, 432, 48), (1, inner_up, 112, 48), (2, first, 112, 48), (3, inner_up, 0, 112), (4, inner_down, 480, 160)]
    return sends, locals_, recvs


def run_exchange(x, moves, nlat, nlon, ident):
    return pl.pallas_call(
        functools.partial(exchange, moves, nlat, nlon),
        in_specs=[pl.BlockSpec(memory_space=pl.ANY)],
        out_specs=pl.BlockSpec(memory_space=pl.ANY),
        out_shape=jax.ShapeDtypeStruct(x.shape, x.dtype),
        scratch_shapes=[pltpu.SemaphoreType.DMA((5,)), pltpu.SemaphoreType.DMA((5,)), pltpu.SemaphoreType.DMA((3,))],
        compiler_params=pltpu.CompilerParams(collective_id=ident, has_side_effects=True),
        name="exchange_out" if ident == 1 else "exchange_back",
    )(x)


def lat_row(lat):
    return ((650 * lat) // 48) * 16


def lon_row(lat, z):
    return ((1300 * lat + 325 * z) // 96) * 16


def x_row(lat, z, x):
    return ((5200 * lat + 1300 * z + 325 * x) // 384) * 16


def al(v):
    return pl.multiple_of(v, 16)


def reduce_kernel(g_ref, m_ref, o_ref, got_core, sum_core, got_z, sum_z, got_y, sum_y, got_x, sum_x, got_l, parts, send_sem, recv_sem):
    lat = lax.axis_index("lat")
    lon = lax.axis_index("lon")
    yh, core = lat // 2, lat % 2
    z, x, yl = lon // 8, (lon // 2) % 4, lon % 2

    def device(yh_, core_, z_, x_, yl_):
        return (yh_ * 2 + core_, z_ * 8 + x_ * 2 + yl_)

    plane = [(dz, dx) for dz in range(4) for dx in range(4) if (dz, dx) != (0, 0)]
    plane_dev = [device(yh, core, (z + dz) % 4, (x + dx) % 4, yl) for dz, dx in plane]
    cube = [(a, c, e) for a in range(2) for c in range(2) for e in range(2) if (a, c, e) != (0, 0, 0)]
    cube_dev = [device((yh + a) % 2, (core + c) % 2, z, x, (yl + e) % 2) for a, c, e in cube]
    greet([(None, d) for d in plane_dev + cube_dev], 22)

    def remote(i, s, d, dev):
        return pltpu.make_async_remote_copy(src_ref=s, dst_ref=d, send_sem=send_sem.at[i], recv_sem=recv_sem.at[i], device_id=dev, device_id_type=MESH)

    def total(*terms):
        out = terms[0].astype(F32)
        for t in terms[1:]:
            out = out + t.astype(F32)
        return out

    pal = device(yh, 1 - core, z, x, yl)
    copies = []
    for h in range(2):
        other = 2 * h + 1 - core
        copies.append(remote(2 * h, g_ref.at[pl.ds(al(576 * other), 576), :], got_core.at[h, pl.ds(0, 576), :], pal))
        copies.append(remote(2 * h + 1, g_ref.at[pl.ds(al(MROWS + lat_row(other)), 240), :], got_core.at[h, pl.ds(576, 240), :], pal))
    for c in copies:
        c.start()
    for c in copies:
        c.wait()
    for h in range(2):
        mine = 2 * h + core
        for t in range(4):
            rows = slice(144 * t, 144 * t + 144)
            sum_core[h, rows, :] = total(g_ref[pl.ds(al(576 * mine + 144 * t), 144), :], got_core[h, rows, :]).astype(BF)
        sum_core[h, 576:816, :] = total(g_ref[pl.ds(al(MROWS + lat_row(mine)), 240), :], got_core[h, 576:816, :]).astype(BF)

    copies = []
    for dz in range(1, 4):
        z_ = (z + dz) % 4
        dev = device(yh, core, z_, x, yl)
        i = 4 + 3 * (dz - 1)
        copies.append(remote(i, sum_core.at[:, pl.ds(al(144 * z_), 144), :], got_z.at[dz - 1, :, pl.ds(0, 144), :], dev))
        for h in range(2):
            lt = 2 * h + core
            copies.append(remote(i + 1 + h, sum_core.at[h, pl.ds(al(576 + lon_row(lt, z_) - lat_row(lt)), 80), :], got_z.at[dz - 1, h, pl.ds(144, 80), :], dev))
    for c in copies:
        c.start()
    for c in copies:
        c.wait()
    for h in range(2):
        lt = 2 * h + core
        own = sum_core[h, pl.ds(al(144 * z), 144), :]
        sum_z[h, 0:144, :] = total(own, *[got_z[t, h, 0:144, :] for t in range(3)]).astype(BF)
        own = sum_core[h, pl.ds(al(576 + lon_row(lt, z) - lat_row(lt)), 80), :]
        sum_z[h, 144:224, :] = total(own, *[got_z[t, h, 144:224, :] for t in range(3)]).astype(BF)

    c = remote(13, sum_z.at[1 - yh], got_y, device(1 - yh, core, z, x, yl))
    c.start()
    c.wait()
    sum_y[...] = total(sum_z[yh], got_y[...]).astype(BF)

    copies = []
    for dx in range(1, 4):
        x_ = (x + dx) % 4
        dev = device(yh, core, z, x_, yl)
        i = 14 + 2 * (dx - 1)
        copies.append(remote(i, sum_y.at[pl.ds(al(32 * x_), 48), :], got_x.at[dx - 1, pl.ds(0, 48), :], dev))
        copies.append(remote(i + 1, sum_y.at[pl.ds(al(144 + x_row(lat, z, x_) - lon_row(lat, z)), 32), :], got_x.at[dx - 1, pl.ds(48, 32), :], dev))
    for c in copies:
        c.start()
    for c in copies:
        c.wait()
    own = sum_y[pl.ds(al(32 * x), 48), :]
    sum_x[0:48, :] = total(own, *[got_x[t, 0:48, :] for t in range(3)]).astype(BF)
    own = sum_y[pl.ds(al(144 + x_row(lat, z, x) - lon_row(lat, z)), 32), :]
    sum_x[48:80, :] = total(own, *[got_x[t, 48:80, :] for t in range(3)]).astype(BF)

    c = remote(20, sum_x, got_l, device(yh, core, z, x, 1 - yl))
    c.start()
    c.wait()
    final = total(sum_x[...], got_l[...])
    matrix, other = final[0:48, :], final[48:80, :]

    first_row = 4 * x + 18 * yl
    row = lax.broadcasted_iota(jnp.int32, (48, 384), 0)
    squares = jnp.where((row >= first_row) & (row < first_row + 18), matrix * matrix, 0.0)
    lane = lax.broadcasted_iota(jnp.int32, (32, 384), 1)
    row = lax.broadcasted_iota(jnp.int32, (32, 384), 0)
    index = (row + x_row(lat, z, x)) * WT + lane - jnp.where(lane >= WT, WT, 0)
    low = 975 * (32 * lat + lon)
    inside = (index >= low) & (index < low + 975) & (lane < 2 * WT)
    squares = jnp.sum(squares, axis=0, keepdims=True) + jnp.sum(jnp.where(inside, other * other, 0.0), axis=0, keepdims=True)
    mine = jnp.sum(squares, axis=1, keepdims=True)

    parts[0] = jnp.broadcast_to(mine, (8, 128))
    copies = [remote(21 + t, parts.at[0], parts.at[1 + t], plane_dev[t]) for t in range(15)]
    for c in copies:
        c.start()
    for c in copies:
        c.wait()
    acc = parts[0]
    for t in range(15):
        acc = acc + parts[1 + t]
    parts[16] = acc
    copies = [remote(36 + t, parts.at[16], parts.at[17 + t], cube_dev[t]) for t in range(7)]
    for c in copies:
        c.start()
    for c in copies:
        c.wait()
    for t in range(7):
        acc = acc + parts[17 + t]
    ceiling = math.sqrt(24 * C * C + 2 * VECB)
    factor = jnp.minimum(1.0, ceiling / (jnp.sqrt(acc) + 1e-06))[0:1, 0:1]
    m_ref[...] = matrix * factor
    o_ref[...] = other * factor


def run_reduce(g):
    slots = 43
    return pl.pallas_call(
        reduce_kernel,
        in_specs=[pl.BlockSpec(memory_space=pltpu.VMEM)],
        out_specs=[pl.BlockSpec(memory_space=pltpu.VMEM)] * 2,
        out_shape=[jax.ShapeDtypeStruct((48, 384), F32), jax.ShapeDtypeStruct((32, 384), F32)],
        scratch_shapes=[
            pltpu.VMEM((2, 816, 384), BF), pltpu.VMEM((2, 816, 384), BF),
            pltpu.VMEM((3, 2, 224, 384), BF), pltpu.VMEM((2, 224, 384), BF),
            pltpu.VMEM((224, 384), BF), pltpu.VMEM((224, 384), BF),
            pltpu.VMEM((3, 80, 384), BF), pltpu.VMEM((80, 384), BF), pltpu.VMEM((80, 384), BF),
            pltpu.VMEM((24, 8, 128), F32),
            pltpu.SemaphoreType.DMA((slots,)), pltpu.SemaphoreType.DMA((slots,)),
        ],
        compiler_params=params(collective_id=3, has_side_effects=True),
        name="reduce_gradient",
    )(g)


def compute_part(nlat, nlon, tokens, cotangent, norm_gains, w_qkv, w_proj, w_up, w_down, pos_bias):
    weights = (norm_gains, w_qkv, w_proj, w_up, w_down, pos_bias.reshape(2, BROWS, WT))
    band = lax.axis_index("lat").astype(jnp.int32).reshape(1)
    *residuals, send = run_first_forward(tokens.reshape(NT, C), cotangent.reshape(NT, C), weights)
    recv = run_exchange(send, moves_out, nlat, nlon, 1)
    back, grad2, dbias2, dg2 = run_second_block(band, recv, weights)
    ret = run_exchange(back, moves_back, nlat, nlon, 2)
    gtok, grad = run_first_backward(ret, weights, residuals, grad2, dbias2, dg2)
    return gtok.reshape(tokens.shape), grad


def shards(nlat, nlon, *args):
    gtok, grad = compute_part(nlat, nlon, *args)
    m, o = run_reduce(grad)
    lat, lon = lax.axis_index("lat"), lax.axis_index("lon")
    z, x, yl = lon // 8, (lon // 2) % 4, lon % 2
    m = lax.dynamic_slice_in_dim(m, 4 * x + 18 * yl, 18, axis=0)
    matrix = m.reshape(18, 2, C).transpose(1, 2, 0)
    flat = o[:, :2 * WT].reshape(32, 2, WT).transpose(1, 0, 2).reshape(2, 32 * WT)
    other = lax.dynamic_slice_in_dim(flat, 975 * (32 * lat + lon) - x_row(lat, z, x) * WT, 975, axis=1)
    return gtok, matrix, other


def solution(mesh):
    grid = P(None, "lat", "lon", None)
    return jax.shard_map(
        functools.partial(shards, mesh.shape["lat"], mesh.shape["lon"]),
        mesh=mesh,
        in_specs=(grid, grid) + (P(),) * 6,
        out_specs=(grid, P(None, None, ("lat", "lon")), P(None, ("lat", "lon"))),
        check_vma=False,
    )
```

time: 542 us -> 134 us (0.25); the launches traced: 532 us -> 134 us
  waiting for transfers between devices: 166 us -> 0 us
  Pallas kernels: 0 us -> 128 us
  local copies, waits for them, and re-layouts: 117 us -> 5.53 us
  matrix products: 80.1 us -> 0 us
  blocking collectives: 63.9 us -> 0 us
  other arithmetic: 60.8 us -> 0 us
  starting transfers between devices: 26.2 us -> 0 us
  between operations: 18 us -> 0.76 us
    unnamed x2 -> x0, waiting for transfers between devices: 155 us -> none
    pallas_call x0 -> x6, Pallas kernels: none -> 128 us  [the longest x1 53.2 us: run_reduce(): pl.pallas_call(reduce_kernel, in_specs=[pl.BlockSpec(memory_space=pltpu.V...]
    dot_general x34 -> x0, matrix products: 69.1 us -> none  [the longest x5 15.3 us: window_attention(): jnp.einsum('nqhd,nkhd->nhqk', packed[:, :, 0], packed[:, :, 1])]
    psum x1 -> x0, blocking collectives: 63.9 us -> none  [shards(): lax.psum(jnp.sum(matrix * matrix) + jnp.sum(remainder * remainder), ('lat...]
    convert_element_type x18 -> x0, local copies, waits for them, and re-layouts: 33.6 us -> none  [the longest x4 14 us: window_attention(): lax.optimization_barrier(packed.astype(jnp.bfloat16)).astype(jnp.float32)]
    reduce_sum x21 -> x0, other arithmetic: 32.4 us -> none  [the longest x8 10.2 us: layer_norm(): return (center * lax.rsqrt(spread + 1e-05) * gain_vec).astype(jnp.bfloat16)]
    reshape x12 -> x3, local copies, waits for them, and re-layouts: 28.6 us -> 1.73 us  [the longest x2 1.02 us: shards(): o[:, :2 * WT].reshape(32, 2, WT).transpose(1, 0, 2).reshape(2, 32 * WT)]
    ppermute x8 -> x0, starting transfers between devices: 26.2 us -> none  [the longest x4 15.7 us: padded(): lax.ppermute(head, axis, [((i + 1) % count, i) for i in range(ends)])]
  transfers between devices with their start and end apart: 9 -> 0, of which waited for: 4 -> 0; matrix products, arithmetic and copies ran while one was open for 2% -> 0% of each run, Pallas kernels for 0% -> 0%
where the time goes in v1:
time: 134 us
  Pallas kernels  128 us (96%)
  local copies, waits for them, and re-layouts  5.53 us (4%)
    pallas_call x1, Pallas kernels, run_reduce(): pl.pallas_call(reduce_kernel, in_specs=[pl.BlockSpec(memory_space=pltpu.V...  53.2 us
    pallas_call x2, Pallas kernels, run_exchange(): pl.pallas_call(functools.partial(exchange, moves, nlat, nlon), in_specs=[...  27.1 us
    pallas_call x1, Pallas kernels, run_second_block(): pl.pallas_call(second_block, grid=(1,), in_specs=[pl.BlockSpec(memory_spa...  20.5 us
    pallas_call x1, Pallas kernels, run_first_backward(): pl.pallas_call(first_backward, grid=(1,), in_specs=[whole((NR, C))] + wei...  15.2 us
    pallas_call x1, Pallas kernels, run_first_forward(): pl.pallas_call(first_forward, grid=(1,), in_specs=[whole((NT, C)), whole(...  11.8 us

profile of v1, /device:TPU:1, one launch (start us, length us, event | category | flops | bytes accessed | tf_op | source)
XLA Modules:
  0.0 134.1 jit_solution(3072243327307423587)
XLA Ops:
  0.7 2.3 %copy.18.wdown_ref = bf16[2,768,192]{2,1,0:T(8,128)(2,1)} copy(bf16[2,768,192]{1,2,0:T(8,128)(2,1)} %param.21) | data formatting | bytes 1179648 | tf_op args[6]
  3.0 11.8 %first_forward.1 = (bf16[576,192]{1,0:T(8,128)(2,1)}, bf16[576,192]{1,0:T(8,128)(2,1)}, bf16[576,192]{1,0:T(8,128)(2,1)}, bf16[576,192]{1,0:T(8,128)(2,1)}, bf16...) custom-call(bf16[576,192]{1,0:T(8,128)(2,1)} %bitcast.11, ...), custom_call_target="tpu_custom_call" | custom-call | tf_op jit(solution)/shard_map/first_forward/pallas_call | solution.py:284
  14.8 17.4 %exchange_out.1.recv_ref = bf16[640,384]{1,0:T(8,128)(2,1)} custom-call(bf16[640,384]{1,0:T(8,128)(2,1)} %get-tuple-element.21.src), custom_call_target="tpu_custom_call" | custom-call | tf_op jit(solution)/shard_map/exchange_out/pallas_call | solution.py:532
  32.1 20.5 %second_block.1 = (bf16[640,192]{1,0:T(8,128)(2,1)}, bf16[2304,256]{1,0:T(8,128)(2,1)}, f32[864,144]{1,0:T(8,128)}, f32[2,192]{1,0:T(2,128)}) custom-call(s32[1]{0:T(128)} %bitcast.band_ref, bf16[640,384]{1,0:T(8,128)(2,1)} %exchange_out.1.recv_ref, f32[2,2,192]{2,1,0:T(2,128)} %gains_ref.5, bf16[2,192,576]{2,1,0:T(8,128)(2,1)} %wqkv_ref.5, ...), custom_call_target="tpu_custom_call" | custom-call | tf_op jit(solution)/shard_map/second_block/pallas_call | solution.py:392
  52.6 9.8 %exchange_back.1.ret_ref = bf16[640,192]{1,0:T(8,128)(2,1)} custom-call(bf16[640,192]{1,0:T(8,128)(2,1)} %get-tuple-element.22.src), custom_call_target="tpu_custom_call" | custom-call | tf_op jit(solution)/shard_map/exchange_back/pallas_call | solution.py:532
  62.4 15.2 %first_backward.1 = (bf16[576,192]{1,0:T(8,128)(2,1)}, bf16[3184,384]{1,0:T(8,128)(2,1)}) custom-call(bf16[640,192]{1,0:T(8,128)(2,1)} %exchange_back.1.ret_ref, f32[2,2,192]{2,1,0:T(2,128)} %gains_ref.5, bf16[2,192,576]{2,1,0:T(8,128)(2,1)} %wqkv_ref.5, bf16[2,192,192]{2,1,0:T(8,128)(2,1)} %wproj_ref.5, bf16[2,192,768]{2,1,0:T(8,128)(2,1)} %wup_ref.5, ...), custom_call_target="tpu_custom_call" | custom-call | tf_op jit(solution)/shard_map/first_backward/pallas_call | solution.py:447
  77.6 53.2 %reduce_gradient.1 = (f32[48,384]{1,0:T(8,128)}, f32[32,384]{1,0:T(8,128)}) custom-call(bf16[3184,384]{1,0:T(8,128)(2,1)} %get-tuple-element.36.g_ref), custom_call_target="tpu_custom_call" | custom-call | tf_op jit(solution)/shard_map/reduce_gradient/pallas_call | solution.py:683
  130.8 0.8 constant_dynamic-slice_fusion.1
  131.6 0.7 reshape.35
  132.3 0.9 reshape.36
  133.3 0.1 reshape.37
  133.4 0.7 constant_dynamic-slice_fusion
  (1 shorter events, 0.0 us)

commit v2 on v0

v2 whole, which is shorter than its diff:
```python
import functools
import math
import types

import jax
import jax.numpy as jnp
import numpy as np
from jax import lax
from jax.experimental import pallas as pl
from jax.experimental.pallas import tpu as pltpu
from jax.sharding import PartitionSpec as P

C = 192
HEADS = 6
HEAD = 32
FFN = 768
WT = 144
NT = 576
NR = 640
QT = 160
MAIN = 112
VECB = 124800
BROWS = HEADS * WT
MROWS = 2304
OROWS = 880
GROWS = MROWS + OROWS
LOG2E = math.log2(math.e)
MESH = pl.DeviceIdType.MESH
BF = jnp.bfloat16
F32 = jnp.float32
VMEM_LIMIT = 56 * 1024 * 1024


def nat(l, r, c):
    return l * 288 + r * 48 + c


def one_hot(sources, width):
    mat = np.zeros((len(sources), width), np.float32)
    for i, s in enumerate(sources):
        if s >= 0:
            mat[i, s] = 1.0
    return mat


@functools.cache
def orders():
    win = [nat(l, r, 12 * w + c) for w in range(4) for l in range(2) for r in range(6) for c in range(12)]

    def cells(rows, cols, size):
        out = [nat(l, r, c) for l in range(2) for r in rows for c in cols]
        return out + [-1] * (size - len(out))

    top, low = range(0, 3), range(3, 6)
    send = []
    for rows in (top, low):
        send += cells(rows, range(0, 18), MAIN)
        send += cells(rows, range(42, 48), QT - MAIN)
        send += cells(rows, range(24, 42), MAIN)
        send += cells(rows, range(18, 24), QT - MAIN)
    slots = []
    for s in range(4):
        for l in range(2):
            for half in range(2):
                for r in range(3):
                    for cc in range(12):
                        col = 12 * (s % 2) + cc
                        base = QT * (2 * (s // 2) + half)
                        if col >= 6:
                            slots.append(base + (l * 3 + r) * 18 + col - 6)
                        else:
                            slots.append(base + MAIN + (l * 3 + r) * 6 + col)
    win_at = {n: i for i, n in enumerate(win)}
    send_win = [win_at[n] if n >= 0 else -1 for n in send]
    to_win = one_hot(win, NT)
    send_from_win = one_hot(send_win, NT)
    send_from_nat = one_hot(send, NT)
    to_slots = one_hot(slots, NR)
    return {
        "to_win": to_win,
        "to_nat": to_win.T.copy(),
        "send_win": send_from_win,
        "win_send": send_from_win.T.copy(),
        "send_nat": send_from_nat,
        "to_slots": to_slots,
        "from_slots": to_slots.T.copy(),
    }


def const(name):
    return jnp.asarray(orders()[name], BF)


def nn(a, b):
    return lax.dot_general(a, b, (((1,), (0,)), ((), ())), preferred_element_type=F32)


def nt(a, b):
    return lax.dot_general(a, b, (((1,), (1,)), ((), ())), preferred_element_type=F32)


def tn(a, b):
    return lax.dot_general(a, b, (((0,), (0,)), ((), ())), preferred_element_type=F32)


def shuffle(mat, x):
    return nn(mat, x).astype(BF)


def stats(x):
    center = x - jnp.mean(x, axis=-1, keepdims=True)
    r = lax.rsqrt(jnp.mean(center * center, axis=-1, keepdims=True) + 1e-05)
    return center * r, r


def norm_back(dn, gain, xhat, r):
    t = dn * gain
    return r * (t - jnp.mean(t, axis=-1, keepdims=True) - xhat * jnp.mean(t * xhat, axis=-1, keepdims=True))


def head_mask(h, dtype):
    lane = lax.broadcasted_iota(jnp.int32, (1, C), 1)
    return ((lane >= h * HEAD) & (lane < (h + 1) * HEAD)).astype(F32).astype(dtype)


def forward_windows(t, b, bias_of, last):
    g0, g1 = t.gains[b, 0:1, :], t.gains[b, 1:2, :]

    def window(w, carry):
        rows = pl.ds(pl.multiple_of(w * WT, WT), WT)
        x = t.x[rows, :].astype(F32)
        u = (stats(x)[0] * g0).astype(BF)
        q = nn(u, t.wq[0]).astype(BF)
        k = nn(u, t.wq[1]).astype(BF)
        v = nn(u, t.wq[2]).astype(BF)
        t.q[rows, :] = q
        t.k[rows, :] = k
        t.v[rows, :] = v
        mixed = jnp.zeros((WT, C), F32)
        for h in range(HEADS):
            s = nt(q * head_mask(h, BF), k) * (HEAD ** -0.5 * LOG2E) + bias_of(w, h)
            e = jnp.exp2(s - jnp.max(s, axis=-1, keepdims=True))
            p = (e * (1.0 / jnp.sum(e, axis=-1, keepdims=True))).astype(BF)
            t.p[pl.ds(pl.multiple_of(w * BROWS + h * WT, WT), WT), :] = p
            mixed = mixed + nn(p, v) * head_mask(h, F32)
        mixed = mixed.astype(BF)
        t.mix[rows, :] = mixed
        attended = nn(mixed, t.w_proj[b]).astype(BF)
        hidden = x + attended.astype(F32)
        t.hid[rows, :] = hidden
        n2 = (stats(hidden)[0] * g1).astype(BF)
        total = hidden
        for j in range(3):
            cols = slice(256 * j, 256 * j + 256)
            up = nn(n2, t.w_up[b, :, cols])
            cdf = 0.5 + 0.5 * lax.erf(up * (0.5 ** 0.5))
            slope = cdf + up * jnp.exp2(up * up * (-0.5 * LOG2E)) * (1.0 / math.sqrt(2 * math.pi))
            act = (up * cdf).astype(BF)
            t.a[rows, cols] = act
            t.gp[rows, cols] = slope.astype(BF)
            if not last:
                total = total + nt(act, t.w_down[b, :, cols])
        if not last:
            t.out[rows, :] = total.astype(BF)
        return carry

    lax.fori_loop(0, 4, window, 0)


def backward_windows(t, b, dbias_of, after_window):
    g0, g1 = t.gains[b, 0:1, :], t.gains[b, 1:2, :]
    t.dg[...] = jnp.zeros((2, C), F32)

    def window(w, carry):
        rows = pl.ds(pl.multiple_of(w * WT, WT), WT)
        dy = t.dout[rows, :]
        dn2 = jnp.zeros((WT, C), F32)
        for j in range(3):
            cols = slice(256 * j, 256 * j + 256)
            da = nn(dy, t.w_down[b, :, cols]).astype(BF).astype(F32)
            dup = (da * t.gp[rows, cols].astype(F32)).astype(BF)
            t.dup[rows, cols] = dup
            dn2 = dn2 + nt(dup, t.w_up[b, :, cols])
        dn2 = dn2.astype(BF).astype(F32)
        xhat, r = stats(t.hid[rows, :])
        t.n2[rows, :] = (xhat * g1).astype(BF)
        t.dg[1:2, :] += jnp.sum(dn2 * xhat, axis=0, keepdims=True)
        dhid = dy.astype(F32) + norm_back(dn2, g1, xhat, r)
        datt = dhid.astype(BF)
        t.datt[rows, :] = datt
        dmix = nt(datt, t.w_proj[b]).astype(BF)
        q = t.q[rows, :]
        k = t.k[rows, :]
        v = t.v[rows, :]
        dq = jnp.zeros((WT, C), F32)
        for h in range(HEADS):
            part = slice(h * WT, h * WT + WT)
            prow = pl.ds(pl.multiple_of(w * BROWS + h * WT, WT), WT)
            dom = dmix * head_mask(h, BF)
            t.dom[part, :] = dom
            t.qm[part, :] = q * head_mask(h, BF)
            dp = nt(dom, v)
            p = t.p[prow, :].astype(F32)
            pd = p * dp
            ds = pd - p * jnp.sum(pd, axis=-1, keepdims=True)
            dbias_of(w, h, ds)
            dsb = ds.astype(BF)
            t.ds[part, :] = dsb
            dq = dq + nn(dsb, k) * head_mask(h, F32)
        pw = t.p[pl.ds(pl.multiple_of(w * BROWS, WT), BROWS), :]
        dq = (dq * HEAD ** -0.5).astype(BF)
        dk = (tn(t.ds[...], t.qm[...]) * HEAD ** -0.5).astype(BF)
        dv = tn(pw, t.dom[...]).astype(BF)
        t.dq[rows, :] = dq
        t.dk[rows, :] = dk
        t.dv[rows, :] = dv
        du = nt(dq, t.wq[0]) + nt(dk, t.wq[1]) + nt(dv, t.wq[2])
        du = du.astype(BF).astype(F32)
        xhat, r = stats(t.x[rows, :].astype(F32))
        t.u[rows, :] = (xhat * g0).astype(BF)
        t.dg[0:1, :] += jnp.sum(du * xhat, axis=0, keepdims=True)
        dx = norm_back(du, g0, xhat, r).astype(BF).astype(F32) + datt.astype(F32)
        t.dx[rows, :] = dx.astype(BF)
        after_window(w)
        return carry

    lax.fori_loop(0, 4, window, 0)


def weight_products(t, part):
    pad = jnp.zeros((NT, 64), BF)

    def left(lhs, x):
        return tn(lhs, jnp.concatenate([x, pad], axis=1))

    def right(lhs, x):
        return tn(lhs, jnp.concatenate([pad, x], axis=1))

    def put(core, row, lft, rgt):
        rows = slice(row, row + lft.shape[0])
        part[core, rows, 0:128] = lft[:, 0:128].astype(BF)
        part[core, rows, 128:256] = (lft[:, 128:256] + rgt[:, 0:128]).astype(BF)
        part[core, rows, 256:384] = rgt[:, 128:256].astype(BF)

    u, n2, dout = t.u[...], t.n2[...], t.dout[...]
    up_low = left(t.dup[:, 0:384], n2)
    up_high = right(t.dup[:, 384:768], n2)
    put(0, 0, left(t.dq[...], u), up_high[0:192])
    put(0, 192, left(t.dk[...], u), up_high[192:384])
    down = right(t.a[:, 0:384], dout)
    put(0, 384, left(t.dv[...], u), down[0:192])
    put(1, 0, left(t.datt[...], t.mix[...]), down[192:384])
    down = right(t.a[:, 384:768], dout)
    put(1, 192, up_low[0:192], down[0:192])
    put(1, 384, up_low[192:384], down[192:384])


def other_rows(t, part):
    flat = jnp.concatenate([t.dg[0:1, :], t.dg[1:2, :], jnp.zeros((1, 3 * WT - 2 * C), F32)], axis=1)
    t.db[BROWS:OROWS, :] = jnp.concatenate([flat[:, 0:WT], flat[:, WT:2 * WT], flat[:, 2 * WT:3 * WT], jnp.zeros((OROWS - BROWS - 3, WT), F32)], axis=0)
    gap = jnp.zeros((240, 48), F32)
    for core in range(2):
        lft = t.db[lat_row(core):lat_row(core) + 240, :]
        rgt = t.db[lat_row(2 + core):lat_row(2 + core) + 240, :]
        part[core, 576:816, :] = jnp.concatenate([lft, gap, rgt, gap], axis=1).astype(BF)


def half_of(shape, axis):
    return (lax.broadcasted_iota(jnp.int32, shape, axis) // 36) % 2


def lane_moves(low):
    src = lax.broadcasted_iota(jnp.int32, (WT, WT), 0)
    dst = lax.broadcasted_iota(jnp.int32, (WT, WT), 1)
    keep = dst - 36 * ((dst // 36) % 2) + (0 if low else 36)
    return (src == keep).astype(F32)


def polar_bias(table, low):
    moved = jnp.dot(table, lane_moves(low), precision=lax.Precision.HIGHEST, preferred_element_type=F32)
    half = half_of((WT, WT), 0)
    if low:
        moved = jnp.where(half == 0, moved, pltpu.roll(moved, 36, 0))
    else:
        moved = jnp.where(half == 1, moved, pltpu.roll(moved, WT - 36, 0))
    return jnp.where(half == half_of((WT, WT), 1), moved, -1e30)


def polar_back(grad, low):
    half = half_of((WT, WT), 0)
    if low:
        folded = jnp.where(half == 0, grad + pltpu.roll(grad, WT - 36, 0), 0.0)
    else:
        folded = jnp.where(half == 1, grad + pltpu.roll(grad, 36, 0), 0.0)
    return lax.dot_general(folded, lane_moves(low), (((1,), (1,)), ((), ())), precision=lax.Precision.HIGHEST, preferred_element_type=F32)


def greet(peers, count):
    barrier = pltpu.get_barrier_semaphore()
    for cond, dev in peers:
        if cond is None:
            pl.semaphore_signal(barrier, inc=1, device_id=dev, device_id_type=MESH)
        else:
            @pl.when(cond)
            def _():
                pl.semaphore_signal(barrier, inc=1, device_id=dev, device_id_type=MESH)
    pl.semaphore_wait(barrier, count)


def guarded(cond, act):
    if cond is None:
        act()
    else:
        pl.when(cond)(act)


class Exchange:
    def __init__(self, moves, src, dst, send_sem, recv_sem, base, here):
        self.sends, self.locals, self.recvs = moves
        self.src, self.dst, self.send_sem, self.recv_sem, self.base, self.here = src, dst, send_sem, recv_sem, base, here

    def remote(self, i, s, d, size, dev):
        return pltpu.make_async_remote_copy(
            src_ref=self.src.at[pl.ds(s, size), :], dst_ref=self.dst.at[pl.ds(d, size), :], send_sem=self.send_sem.at[self.base + i],
            recv_sem=self.recv_sem.at[self.base + i], device_id=dev, device_id_type=MESH)

    def start(self):
        for i, cond, s, d, size, dev in self.sends:
            guarded(cond, lambda: self.remote(i, s, d, size, dev).start())
        for cond, s, d, size in self.locals:
            def keep():
                self.dst[d:d + size, :] = self.src[s:s + size, :]
            guarded(cond, keep)

    def finish(self):
        for i, cond, d, size in self.recvs:
            guarded(cond, lambda: self.remote(i, 0, d, size, self.here).wait_recv())
        for i, cond, s, d, size, dev in self.sends:
            guarded(cond, lambda: self.remote(i, s, d, size, dev).wait_send())


def moves_out(n):
    sends = [
        (0, None, 432, 432, 48, (n.b, n.east)),
        (1, n.inner_up, 112, 592, 48, (n.up, n.east)),
        (2, n.first, 112, 112, 48, (n.b, n.east)),
        (3, n.inner_up, 0, 480, 112, (n.up, n.j)),
        (4, n.inner_down, 480, 0, 160, (n.down, n.j)),
    ]
    locals_ = [(None, 160, 160, 272), (n.first, 0, 0, 112), (n.last, 480, 480, 160)]
    recvs = [(0, None, 432, 48), (1, n.inner_down, 592, 48), (2, n.first, 112, 48), (3, n.inner_down, 480, 112), (4, n.inner_up, 0, 160)]
    return sends, locals_, recvs


def moves_back(n):
    sends = [
        (0, None, 432, 432, 48, (n.b, n.west)),
        (1, n.inner_down, 592, 112, 48, (n.down, n.west)),
        (2, n.first, 112, 112, 48, (n.b, n.west)),
        (3, n.inner_down, 480, 0, 112, (n.down, n.j)),
        (4, n.inner_up, 0, 480, 160, (n.up, n.j)),
    ]
    locals_ = [(None, 160, 160, 272), (n.first, 0, 0, 112), (n.last, 480, 480, 160)]
    recvs = [(0, None, 432, 48), (1, n.inner_up, 112, 48), (2, n.first, 112, 48), (3, n.inner_up, 0, 112), (4, n.inner_down, 480, 160)]
    return sends, locals_, recvs


def lat_row(lat):
    return ((650 * lat) // 48) * 16


def z_row(core, z):
    return ((52 * core + 325 * z) // 96) * 16


def x_row(lat, z, x):
    return ((5200 * lat + 1300 * z + 325 * x) // 384) * 16


def al(v):
    return pl.multiple_of(v, 16)


def total(*terms):
    out = terms[0].astype(F32)
    for term in terms[1:]:
        out = out + term.astype(F32)
    return out


class Reduce:
    def __init__(self, n, t, send_sem, recv_sem, base):
        self.n, self.t, self.send_sem, self.recv_sem, self.base = n, t, send_sem, recv_sem, base

    def remote(self, i, s, d, dev):
        i = self.base + i
        return pltpu.make_async_remote_copy(src_ref=s, dst_ref=d, send_sem=self.send_sem.at[i], recv_sem=self.recv_sem.at[i], device_id=dev, device_id_type=MESH)

    def core_copies(self):
        n, t = self.n, self.t
        return [self.remote(0, t.part.at[1 - n.core], t.got_core, n.device(core=1 - n.core))]

    def z_copies(self):
        n, t = self.n, self.t
        out = []
        for d in range(1, 4):
            z = (n.z + d) % 4
            dev = n.device(z=z)
            out.append(self.remote(2 * d - 1, t.sum_core.at[pl.ds(al(144 * z), 144), :], t.got_z.at[d - 1, pl.ds(0, 144), :], dev))
            out.append(self.remote(2 * d, t.sum_core.at[pl.ds(al(576 + z_row(n.core, z)), 80), :], t.got_z.at[d - 1, pl.ds(144, 80), :], dev))
        return out

    def y_copies(self):
        n, t = self.n, self.t
        return [self.remote(7, t.sum_z.at[:, pl.ds(pl.multiple_of(128 * (1 - n.yh), 128), 256)], t.got_y, n.device(yh=1 - n.yh))]

    def x_window(self, x):
        n = self.n
        return al(144 + x_row(n.b, n.z, x) - lat_row(n.b) - z_row(n.core, n.z))

    def x_copies(self):
        n, t = self.n, self.t
        out = []
        for d in range(1, 4):
            x = (n.x + d) % 4
            dev = n.device(x=x)
            out.append(self.remote(6 + 2 * d, t.sum_y.at[pl.ds(al(32 * x), 48), :], t.got_x.at[d - 1, pl.ds(0, 48), :], dev))
            out.append(self.remote(7 + 2 * d, t.sum_y.at[pl.ds(self.x_window(x), 32), :], t.got_x.at[d - 1, pl.ds(48, 32), :], dev))
        return out

    def l_copies(self):
        return [self.remote(14, self.t.sum_x, self.t.got_l, self.n.device(yl=1 - self.n.yl))]

    def start(self, copies):
        for c in copies:
            c.start()

    def wait(self, copies):
        for c in copies:
            c.wait()

    def core_start(self):
        self.start(self.core_copies())

    def core_to_z(self):
        n, t = self.n, self.t
        self.wait(self.core_copies())
        for i in range(3):
            rows = slice(272 * i, 272 * i + 272)
            t.sum_core[rows, :] = total(t.part[n.core, rows, :], t.got_core[rows, :]).astype(BF)
        self.start(self.z_copies())

    def z_to_y(self):
        n, t = self.n, self.t
        self.wait(self.z_copies())
        own = t.sum_core[pl.ds(al(144 * n.z), 144), :]
        t.sum_z[0:144, :] = total(own, *[t.got_z[i, 0:144, :] for i in range(3)]).astype(BF)
        own = t.sum_core[pl.ds(al(576 + z_row(n.core, n.z)), 80), :]
        t.sum_z[144:224, :] = total(own, *[t.got_z[i, 144:224, :] for i in range(3)]).astype(BF)
        self.start(self.y_copies())

    def y_to_x(self):
        n, t = self.n, self.t
        self.wait(self.y_copies())
        own = t.sum_z[:, pl.ds(pl.multiple_of(128 * n.yh, 128), 256)]
        t.sum_y[...] = total(own, t.got_y[...]).astype(BF)
        self.start(self.x_copies())

    def x_to_l(self):
        n, t = self.n, self.t
        self.wait(self.x_copies())
        own = t.sum_y[pl.ds(al(32 * n.x), 48), :]
        t.sum_x[0:48, :] = total(own, *[t.got_x[i, 0:48, :] for i in range(3)]).astype(BF)
        own = t.sum_y[pl.ds(self.x_window(n.x), 32), :]
        t.sum_x[48:80, :] = total(own, *[t.got_x[i, 48:80, :] for i in range(3)]).astype(BF)
        self.start(self.l_copies())

    def finish(self):
        self.wait(self.l_copies())
        final = total(self.t.sum_x[...], self.t.got_l[...])
        return jnp.where(self.n.yh == 1, pltpu.roll(final, 192, 1), final)


def share_squares(n, final):
    matrix, other = final[0:48, :], final[48:80, :]
    row = lax.broadcasted_iota(jnp.int32, (48, 256), 0)
    lane = lax.broadcasted_iota(jnp.int32, (48, 256), 1)
    low = 4 * n.x + 18 * n.yl
    squares = jnp.sum(jnp.where((row >= low) & (row < low + 18) & (lane < C), matrix * matrix, 0.0), axis=0, keepdims=True)
    row = lax.broadcasted_iota(jnp.int32, (32, 256), 0)
    lane = lax.broadcasted_iota(jnp.int32, (32, 256), 1)
    index = (row + x_row(n.b, n.z, n.x)) * WT + lane
    low = 975 * (32 * n.b + n.j)
    inside = (index >= low) & (index < low + 975) & (lane < WT)
    squares = squares + jnp.sum(jnp.where(inside, other * other, 0.0), axis=0, keepdims=True)
    return jnp.sum(squares, axis=1, keepdims=True)


INPUTS = ["tok", "cot", "gains", "w_qkv", "w_proj", "w_up", "w_down", "bias", "to_win", "to_nat", "send_win", "win_send", "send_nat", "to_slots", "from_slots"]
PERMS = INPUTS[8:]
OUTPUTS = [("gtok", (NT, C), BF), ("m", (2, 48, 256), F32), ("o", (2, 32, 256), F32)]
BLOCK = [
    ("x", (NT, C), BF), ("wq", (3, C, C), BF), ("q", (NT, C), BF), ("k", (NT, C), BF), ("v", (NT, C), BF), ("p", (4 * BROWS, WT), BF),
    ("mix", (NT, C), BF), ("hid", (NT, C), F32), ("a", (NT, FFN), BF), ("gp", (NT, FFN), BF), ("dout", (NT, C), BF), ("part", (2, 816, 384), BF),
    ("got_core", (816, 384), BF), ("sum_core", (816, 384), BF), ("got_z", (3, 224, 384), BF), ("sum_z", (224, 384), BF),
    ("got_y", (224, 256), BF), ("sum_y", (224, 256), BF), ("got_x", (3, 80, 256), BF), ("sum_x", (80, 256), BF), ("got_l", (80, 256), BF),
    ("db", (OROWS, WT), F32), ("dg", (2, C), F32),
]
SHARED = [
    ("out", (NT, C), BF), ("dx", (NT, C), BF), ("u", (NT, C), BF), ("n2", (NT, C), BF), ("datt", (NT, C), BF), ("dq", (NT, C), BF), ("dk", (NT, C), BF),
    ("dv", (NT, C), BF), ("dup", (NT, FFN), BF), ("dom", (BROWS, C), BF), ("qm", (BROWS, C), BF), ("ds", (BROWS, WT), BF),
    ("lbias", (3, BROWS, WT), F32), ("db_b", (BROWS, WT), F32), ("parts", (24, 8, 128), F32),
    ("cot_src", (NR, C), BF), ("cot_dst", (NR, C), BF), ("mid_src", (NR, C), BF), ("mid_dst", (NR, C), BF), ("back_src", (NR, C), BF), ("back_dst", (NR, C), BF),
]
SEMS = 15 + 30 + 22


def place(nlat, nlon):
    n = types.SimpleNamespace()
    n.b, n.j = lax.axis_index("lat"), lax.axis_index("lon")
    n.east, n.west = lax.rem(n.j + 1, nlon), lax.rem(n.j + nlon - 1, nlon)
    n.up, n.down = jnp.maximum(n.b - 1, 0), jnp.minimum(n.b + 1, nlat - 1)
    n.first, n.last = n.b == 0, n.b == nlat - 1
    n.inner_up, n.inner_down = n.b > 0, n.b < nlat - 1
    n.yh, n.core = n.b // 2, n.b % 2
    n.z, n.x, n.yl = n.j // 8, (n.j // 2) % 4, n.j % 2

    def device(yh=n.yh, core=n.core, z=n.z, x=n.x, yl=n.yl):
        return (yh * 2 + core, z * 8 + x * 2 + yl)

    n.device = device
    return n


def kernel(nlat, nlon, reduce, *refs):
    names = INPUTS + [o[0] for o in OUTPUTS] + ["first_" + e[0] for e in BLOCK] + ["second_" + e[0] for e in BLOCK] + [e[0] for e in SHARED] + ["send_sem", "recv_sem"]
    r = dict(zip(names, refs, strict=True))
    weights = {k: r[k] for k in INPUTS}
    blocks = []
    for label in ("first_", "second_"):
        blocks.append(types.SimpleNamespace(**weights, **{e[0]: r[e[0]] for e in SHARED}, **{e[0]: r[label + e[0]] for e in BLOCK}))
    one, two = blocks
    n = place(nlat, nlon)
    sems = (r["send_sem"], r["recv_sem"])
    here = (n.b, n.j)
    ex_cot = Exchange(moves_out(n), one.cot_src, one.cot_dst, *sems, 0, here)
    ex_mid = Exchange(moves_out(n), one.mid_src, one.mid_dst, *sems, 5, here)
    ex_back = Exchange(moves_back(n), one.back_src, one.back_dst, *sems, 10, here)

    plane = [(dz, dx) for dz in range(4) for dx in range(4) if (dz, dx) != (0, 0)]
    plane_dev = [n.device(z=(n.z + dz) % 4, x=(n.x + dx) % 4) for dz, dx in plane]
    cube = [(a, c, e) for a in range(2) for c in range(2) for e in range(2) if (a, c, e) != (0, 0, 0)]
    cube_dev = [n.device(yh=(n.yh + a) % 2, core=(n.core + c) % 2, yl=(n.yl + e) % 2) for a, c, e in cube]
    far = plane_dev + cube_dev if reduce else []
    greet(
        [(None, (n.b, n.east)), (None, (n.b, n.west)), (n.inner_up, (n.up, n.j)), (n.inner_down, (n.down, n.j)), (n.inner_up, (n.up, n.east)), (n.inner_down, (n.down, n.west))]
        + [(None, d) for d in far],
        jnp.where(jnp.logical_or(n.first, n.last), 4, 6) + len(far),
    )

    one.cot_src[...] = shuffle(one.send_nat[...], one.cot[...])
    ex_cot.start()
    one.x[...] = shuffle(one.to_win[...], one.tok[...])
    for b, t in enumerate(blocks):
        for i in range(3):
            t.wq[i] = t.w_qkv[b, :, C * i:C * i + C]
    one.lbias[0] = one.bias[0] * LOG2E
    forward_windows(one, 0, lambda w, h: one.lbias[0, h * WT:h * WT + WT, :], False)
    one.mid_src[...] = shuffle(one.send_win[...], one.out[...])
    ex_mid.start()

    for group in range(2):
        polar = n.first if group == 0 else n.last

        @pl.when(polar)
        def _():
            for h in range(HEADS):
                rows = slice(h * WT, h * WT + WT)
                two.lbias[1 + group, rows, :] = polar_bias(two.bias[1, rows, :] * LOG2E, group == 1)

        @pl.when(jnp.logical_not(polar))
        def _():
            two.lbias[1 + group] = two.bias[1] * LOG2E

    two.db[...] = jnp.zeros((OROWS, WT), F32)
    two.db_b[...] = jnp.zeros((BROWS, WT), F32)
    ex_cot.finish()
    two.dout[...] = shuffle(two.to_slots[...], two.cot_dst[...])
    ex_mid.finish()
    two.x[...] = shuffle(two.to_slots[...], two.mid_dst[...])
    forward_windows(two, 1, lambda w, h: two.lbias[1 + w // 2, h * WT:h * WT + WT, :], True)

    def dbias_two(w, h, ds):
        rows = slice(h * WT, h * WT + WT)

        @pl.when(w < 2)
        def _():
            two.db[rows, :] += ds

        @pl.when(w >= 2)
        def _():
            two.db_b[rows, :] += ds

    backward_windows(two, 1, dbias_two, lambda w: None)
    two.back_src[...] = shuffle(two.from_slots[...], two.dx[...])
    ex_back.start()
    for group, ref in enumerate((two.db, two.db_b)):
        @pl.when(n.first if group == 0 else n.last)
        def _():
            for h in range(HEADS):
                rows = slice(h * WT, h * WT + WT)
                ref[rows, :] = polar_back(ref[rows, :], group == 1)

    two.db[0:BROWS, :] += two.db_b[...]
    weight_products(two, two.part)
    other_rows(two, two.part)
    red_one = Reduce(n, one, *sems, 15)
    red_two = Reduce(n, two, *sems, 30)
    if reduce:
        red_two.core_start()

    ex_back.finish()
    one.dout[...] = shuffle(one.win_send[...], one.back_dst[...])
    one.db[...] = jnp.zeros((OROWS, WT), F32)

    def dbias_one(w, h, ds):
        one.db[h * WT:h * WT + WT, :] += ds

    def step(w):
        if reduce:
            pl.when(w == 0)(red_two.core_to_z)
            pl.when(w == 2)(red_two.z_to_y)
            pl.when(w == 3)(red_two.y_to_x)

    backward_windows(one, 0, dbias_one, step)
    weight_products(one, one.part)
    other_rows(one, one.part)
    if reduce:
        red_one.core_start()
    r["gtok"][...] = shuffle(one.to_nat[...], one.dx[...])
    if not reduce:
        return
    red_two.x_to_l()
    red_one.core_to_z()
    two_final = red_two.finish()
    red_one.z_to_y()
    red_one.y_to_x()
    red_one.x_to_l()
    one_final = red_one.finish()

    parts = one.parts
    parts[0] = jnp.broadcast_to(share_squares(n, one_final) + share_squares(n, two_final), (8, 128))

    def spread(base, source, target, devices):
        copies = [
            pltpu.make_async_remote_copy(src_ref=parts.at[source], dst_ref=parts.at[target + i], send_sem=sems[0].at[base + i], recv_sem=sems[1].at[base + i], device_id=d, device_id_type=MESH)
            for i, d in enumerate(devices)
        ]
        for c in copies:
            c.start()
        for c in copies:
            c.wait()
        acc = parts[source]
        for i in range(len(devices)):
            acc = acc + parts[target + i]
        return acc

    parts[16] = spread(45, 0, 1, plane_dev)
    acc = spread(60, 16, 17, cube_dev)
    ceiling = math.sqrt(24 * C * C + 2 * VECB)
    factor = jnp.minimum(1.0, ceiling / (jnp.sqrt(acc) + 1e-06))[0:1, 0:1]
    for b, final in enumerate((one_final, two_final)):
        r["m"][b] = final[0:48, :] * factor
        r["o"][b] = final[48:80, :] * factor


def run(nlat, nlon, reduce, tokens, cotangent, norm_gains, w_qkv, w_proj, w_up, w_down, pos_bias):
    args = [tokens.reshape(NT, C), cotangent.reshape(NT, C), norm_gains, w_qkv, w_proj, w_up, jnp.swapaxes(w_down, 1, 2), pos_bias.reshape(2, BROWS, WT)]
    args += [const(p) for p in PERMS]
    vmem = pl.BlockSpec(memory_space=pltpu.VMEM)
    return pl.pallas_call(
        functools.partial(kernel, nlat, nlon, reduce),
        in_specs=[vmem] * len(args),
        out_specs=[vmem] * len(OUTPUTS),
        out_shape=[jax.ShapeDtypeStruct(s, d) for _, s, d in OUTPUTS],
        scratch_shapes=[pltpu.VMEM(s, d) for _, s, d in BLOCK + BLOCK + SHARED] + [pltpu.SemaphoreType.DMA((SEMS,))] * 2,
        compiler_params=pltpu.CompilerParams(vmem_limit_bytes=VMEM_LIMIT, collective_id=1, has_side_effects=True),
        name="two_blocks",
    )(*args)


def shards(nlat, nlon, tokens, *args):
    gtok, m, o = run(nlat, nlon, True, tokens, *args)
    n = place(nlat, nlon)
    m = lax.dynamic_slice_in_dim(m, 4 * n.x + 18 * n.yl, 18, axis=1)[:, :, :C]
    flat = o[:, :, :WT].reshape(2, 32 * WT)
    other = lax.dynamic_slice_in_dim(flat, 975 * (32 * n.b + n.j) - x_row(n.b, n.z, n.x) * WT, 975, axis=1)
    return gtok.reshape(tokens.shape), m.transpose(0, 2, 1), other


def solution(mesh):
    grid = P(None, "lat", "lon", None)
    return jax.shard_map(
        functools.partial(shards, mesh.shape["lat"], mesh.shape["lon"]),
        mesh=mesh,
        in_specs=(grid, grid) + (P(),) * 6,
        out_specs=(grid, P(None, None, ("lat", "lon")), P(None, ("lat", "lon"))),
        check_vma=False,
    )
```

time: 542 us -> 112 us (0.21); the launches traced: 532 us -> 112 us
  waiting for transfers between devices: 166 us -> 0 us
  local copies, waits for them, and re-layouts: 117 us -> 4.82 us
  Pallas kernels: 0 us -> 106 us
  matrix products: 80.1 us -> 0 us
  blocking collectives: 63.9 us -> 0 us
  other arithmetic: 60.8 us -> 0 us
  starting transfers between devices: 26.2 us -> 0 us
  between operations: 18 us -> 0.71 us
    unnamed x2 -> x0, waiting for transfers between devices: 155 us -> none
    pallas_call x0 -> x1, Pallas kernels: none -> 106 us  [run(): pl.pallas_call(functools.partial(kernel, nlat, nlon, reduce), in_specs=[v...]
    dot_general x34 -> x0, matrix products: 69.1 us -> none  [the longest x5 15.3 us: window_attention(): jnp.einsum('nqhd,nkhd->nhqk', packed[:, :, 0], packed[:, :, 1])]
    psum x1 -> x0, blocking collectives: 63.9 us -> none  [shards(): lax.psum(jnp.sum(matrix * matrix) + jnp.sum(remainder * remainder), ('lat...]
    convert_element_type x18 -> x0, local copies, waits for them, and re-layouts: 33.6 us -> none  [the longest x4 14 us: window_attention(): lax.optimization_barrier(packed.astype(jnp.bfloat16)).astype(jnp.float32)]
    reduce_sum x21 -> x0, other arithmetic: 32.4 us -> none  [the longest x8 10.2 us: layer_norm(): return (center * lax.rsqrt(spread + 1e-05) * gain_vec).astype(jnp.bfloat16)]
    reshape x12 -> x1, local copies, waits for them, and re-layouts: 28.6 us -> 0.96 us  [shards(): flat = o[:, :, :WT].reshape(2, 32 * WT)]
    ppermute x8 -> x0, starting transfers between devices: 26.2 us -> none  [the longest x4 15.7 us: padded(): lax.ppermute(head, axis, [((i + 1) % count, i) for i in range(ends)])]
  transfers between devices with their start and end apart: 9 -> 0, of which waited for: 4 -> 0; matrix products, arithmetic and copies ran while one was open for 2% -> 0% of each run, Pallas kernels for 0% -> 0%
where the time goes in v2:
time: 112 us
  Pallas kernels  106 us (95%)
  local copies, waits for them, and re-layouts  4.82 us (4%)
    pallas_call x1, Pallas kernels, run(): pl.pallas_call(functools.partial(kernel, nlat, nlon, reduce), in_specs=[v...  106 us
    unnamed x2, local copies, waits for them, and re-layouts  2.33 us

profile of v2, /device:TPU:1, one launch (start us, length us, event | category | flops | bytes accessed | tf_op | source)
XLA Modules:
  0.0 111.6 jit_solution(3357842149038135563)
XLA Ops:
  0.7 106.1 %two_blocks.1 = (bf16[576,192]{1,0:T(8,128)(2,1)}, f32[2,48,256]{2,1,0:T(8,128)}, f32[2,32,256]{2,1,0:T(8,128)}) custom-call(bf16[576,192]{1,0:T(8,128)(2,1)} %bitcast.10, bf16[576,192]{1,0:T(8,128)(2,1)} %bitcast.11, f32[2,2,192]{2,1,0:T(2,128)} %refs_2_.1, bf16[2,192,576]{2,1,0:T(8,128)(2,1)} %refs_3_.1, bf16[2,192,192]{2,1,0:T(8,128)(2,1)} %refs_4_.1, ...), custom_call_target="tpu_custom_call" | custom-call | tf_op jit(solution)/shard_map/two_blocks/pallas_call | solution.py:681
  106.8 1.0 reshape.25
  107.8 0.7 constant_dynamic-slice_fusion
  108.4 0.8 dynamic-slice_bitcast_fusion
  109.3 0.6 copy.18
  109.9 1.7 %copy.20 = bf16[2,6,48,192]{3,2,1,0:T(8,128)(2,1)} copy(bf16[2,6,48,192]{3,2,1,0:T(8,128)(2,1)} %bitcast.12) | data formatting | bytes 442368

commit v3 on v2

--- a/solution.py
+++ b/solution.py
@@ -164,7 +164,7 @@
             t.out[rows, :] = total.astype(BF)
         return carry
 
-    lax.fori_loop(0, 4, window, 0)
+    lax.fori_loop(0, 4, window, 0, unroll=2)
 
 
 def backward_windows(t, b, dbias_of, after_window):
@@ -192,25 +192,26 @@
         q = t.q[rows, :]
         k = t.k[rows, :]
         v = t.v[rows, :]
-        dq = jnp.zeros((WT, C), F32)
+        doms = jnp.concatenate([dmix * head_mask(h, BF) for h in range(HEADS)], axis=0)
+        qms = jnp.concatenate([q * head_mask(h, BF) for h in range(HEADS)], axis=0)
+        dps = nt(doms, v)
+        pw = t.p[pl.ds(pl.multiple_of(w * BROWS, WT), BROWS), :]
+        dss = []
         for h in range(HEADS):
             part = slice(h * WT, h * WT + WT)
-            prow = pl.ds(pl.multiple_of(w * BROWS + h * WT, WT), WT)
-            dom = dmix * head_mask(h, BF)
-            t.dom[part, :] = dom
-            t.qm[part, :] = q * head_mask(h, BF)
-            dp = nt(dom, v)
-            p = t.p[prow, :].astype(F32)
-            pd = p * dp
+            p = pw[part].astype(F32)
+            pd = p * dps[part]
             ds = pd - p * jnp.sum(pd, axis=-1, keepdims=True)
             dbias_of(w, h, ds)
-            dsb = ds.astype(BF)
-            t.ds[part, :] = dsb
-            dq = dq + nn(dsb, k) * head_mask(h, F32)
-        pw = t.p[pl.ds(pl.multiple_of(w * BROWS, WT), BROWS), :]
+            dss.append(ds.astype(BF))
+        dss = jnp.concatenate(dss, axis=0)
+        dqs = nn(dss, k)
+        dq = dqs[0:WT] * head_mask(0, F32)
+        for h in range(1, HEADS):
+            dq = dq + dqs[h * WT:h * WT + WT] * head_mask(h, F32)
         dq = (dq * HEAD ** -0.5).astype(BF)
-        dk = (tn(t.ds[...], t.qm[...]) * HEAD ** -0.5).astype(BF)
-        dv = tn(pw, t.dom[...]).astype(BF)
+        dk = (tn(dss, qms) * HEAD ** -0.5).astype(BF)
+        dv = tn(pw, doms).astype(BF)
         t.dq[rows, :] = dq
         t.dk[rows, :] = dk
         t.dv[rows, :] = dv
@@ -224,7 +225,7 @@
         after_window(w)
         return carry
 
-    lax.fori_loop(0, 4, window, 0)
+    lax.fori_loop(0, 4, window, 0, unroll=2)
 
 
 def weight_products(t, part):
@@ -295,7 +296,7 @@
     return lax.dot_general(folded, lane_moves(low), (((1,), (1,)), ((), ())), precision=lax.Precision.HIGHEST, preferred_element_type=F32)
 
 
-def greet(peers, count):
+def greet(peers):
     barrier = pltpu.get_barrier_semaphore()
     for cond, dev in peers:
         if cond is None:
@@ -304,7 +305,6 @@
             @pl.when(cond)
             def _():
                 pl.semaphore_signal(barrier, inc=1, device_id=dev, device_id_type=MESH)
-    pl.semaphore_wait(barrier, count)
 
 
 def guarded(cond, act):
@@ -373,8 +373,8 @@
     return ((52 * core + 325 * z) // 96) * 16
 
 
-def x_row(lat, z, x):
-    return ((5200 * lat + 1300 * z + 325 * x) // 384) * 16
+def x_row(core, z, x):
+    return ((208 * core + 1300 * z + 325 * x) // 384) * 16
 
 
 def al(v):
@@ -400,36 +400,39 @@
         n, t = self.n, self.t
         return [self.remote(0, t.part.at[1 - n.core], t.got_core, n.device(core=1 - n.core))]
 
-    def z_copies(self):
+    def first_copies(self):
         n, t = self.n, self.t
         out = []
         for d in range(1, 4):
+            i = 3 * d - 2
             z = (n.z + d) % 4
+            x = (n.x + d) % 4
+            out.append(self.remote(i, t.sum_m.at[:, pl.ds(al(32 * x), 48), pl.ds(128, 256)], t.got_x.at[d - 1], n.device(x=x)))
             dev = n.device(z=z)
-            out.append(self.remote(2 * d - 1, t.sum_core.at[pl.ds(al(144 * z), 144), :], t.got_z.at[d - 1, pl.ds(0, 144), :], dev))
-            out.append(self.remote(2 * d, t.sum_core.at[pl.ds(al(576 + z_row(n.core, z)), 80), :], t.got_z.at[d - 1, pl.ds(144, 80), :], dev))
+            out.append(self.remote(i + 1, t.sum_o.at[pl.ds(al(z_row(n.core, z)), 80), :], t.got_o.at[d - 1], dev))
+            out.append(self.remote(i + 2, t.sum_m.at[z, :, pl.ds(0, 128)], t.got_z.at[d - 1], dev))
         return out
 
-    def y_copies(self):
-        n, t = self.n, self.t
-        return [self.remote(7, t.sum_z.at[:, pl.ds(pl.multiple_of(128 * (1 - n.yh), 128), 256)], t.got_y, n.device(yh=1 - n.yh))]
-
     def x_window(self, x):
-        n = self.n
-        return al(144 + x_row(n.b, n.z, x) - lat_row(n.b) - z_row(n.core, n.z))
-
-    def x_copies(self):
+        return al(x_row(self.n.core, self.n.z, x) - z_row(self.n.core, self.n.z))
+
+    def second_copies(self):
         n, t = self.n, self.t
         out = []
         for d in range(1, 4):
+            i = 3 * d + 7
+            z = (n.z + d) % 4
             x = (n.x + d) % 4
+            out.append(self.remote(i, t.sum_x.at[z], t.got_xz.at[d - 1], n.device(z=z)))
             dev = n.device(x=x)
-            out.append(self.remote(6 + 2 * d, t.sum_y.at[pl.ds(al(32 * x), 48), :], t.got_x.at[d - 1, pl.ds(0, 48), :], dev))
-            out.append(self.remote(7 + 2 * d, t.sum_y.at[pl.ds(self.x_window(x), 32), :], t.got_x.at[d - 1, pl.ds(48, 32), :], dev))
+            out.append(self.remote(i + 1, t.sum_zo.at[pl.ds(self.x_window(x), 32), :], t.got_ox.at[d - 1], dev))
+            out.append(self.remote(i + 2, t.sum_z.at[pl.ds(al(32 * x), 48), :], t.got_zx.at[d - 1], dev))
         return out
 
-    def l_copies(self):
-        return [self.remote(14, self.t.sum_x, self.t.got_l, self.n.device(yl=1 - self.n.yl))]
+    def third_copies(self):
+        n, t = self.n, self.t
+        devices = [n.device(yl=1 - n.yl), n.device(yh=1 - n.yh), n.device(yl=1 - n.yl, yh=1 - n.yh)]
+        return [self.remote(19 + i, t.mid, t.got_y.at[i], dev) for i, dev in enumerate(devices)]
 
     def start(self, copies):
         for c in copies:
@@ -442,58 +445,55 @@
     def core_start(self):
         self.start(self.core_copies())
 
-    def core_to_z(self):
+    def core_to_first(self):
         n, t = self.n, self.t
         self.wait(self.core_copies())
-        for i in range(3):
-            rows = slice(272 * i, 272 * i + 272)
-            t.sum_core[rows, :] = total(t.part[n.core, rows, :], t.got_core[rows, :]).astype(BF)
-        self.start(self.z_copies())
-
-    def z_to_y(self):
+        for z in range(4):
+            rows = slice(144 * z, 144 * z + 144)
+            t.sum_m[z] = total(t.part[n.core, rows, :], t.got_core[rows, :]).astype(BF)
+        t.sum_o[...] = total(t.part[n.core, 576:816, :], t.got_core[576:816, :]).astype(BF)
+        self.start(self.first_copies())
+
+    def first_to_second(self):
         n, t = self.n, self.t
-        self.wait(self.z_copies())
-        own = t.sum_core[pl.ds(al(144 * n.z), 144), :]
-        t.sum_z[0:144, :] = total(own, *[t.got_z[i, 0:144, :] for i in range(3)]).astype(BF)
-        own = t.sum_core[pl.ds(al(576 + z_row(n.core, n.z)), 80), :]
-        t.sum_z[144:224, :] = total(own, *[t.got_z[i, 144:224, :] for i in range(3)]).astype(BF)
-        self.start(self.y_copies())
-
-    def y_to_x(self):
+        self.wait(self.first_copies())
+        t.sum_x[...] = total(t.sum_m[:, pl.ds(al(32 * n.x), 48), 128:384], *[t.got_x[i] for i in range(3)]).astype(BF)
+        t.sum_zo[...] = total(t.sum_o[pl.ds(al(z_row(n.core, n.z)), 80), :], *[t.got_o[i] for i in range(3)]).astype(BF)
+        t.sum_z[...] = total(t.sum_m[n.z, :, 0:128], *[t.got_z[i] for i in range(3)]).astype(BF)
+        self.start(self.second_copies())
+
+    def second_to_third(self):
         n, t = self.n, self.t
-        self.wait(self.y_copies())
-        own = t.sum_z[:, pl.ds(pl.multiple_of(128 * n.yh, 128), 256)]
-        t.sum_y[...] = total(own, t.got_y[...]).astype(BF)
-        self.start(self.x_copies())
-
-    def x_to_l(self):
-        n, t = self.n, self.t
-        self.wait(self.x_copies())
-        own = t.sum_y[pl.ds(al(32 * n.x), 48), :]
-        t.sum_x[0:48, :] = total(own, *[t.got_x[i, 0:48, :] for i in range(3)]).astype(BF)
-        own = t.sum_y[pl.ds(self.x_window(n.x), 32), :]
-        t.sum_x[48:80, :] = total(own, *[t.got_x[i, 48:80, :] for i in range(3)]).astype(BF)
-        self.start(self.l_copies())
+        self.wait(self.second_copies())
+        t.mid[0:48, 0:128] = total(t.sum_z[pl.ds(al(32 * n.x), 48), :], *[t.got_zx[i] for i in range(3)]).astype(BF)
+        t.mid[0:48, 128:384] = total(t.sum_x[n.z], *[t.got_xz[i] for i in range(3)]).astype(BF)
+        t.mid[48:80, :] = total(t.sum_zo[pl.ds(self.x_window(n.x), 32), :], *[t.got_ox[i] for i in range(3)]).astype(BF)
+        self.start(self.third_copies())
 
     def finish(self):
-        self.wait(self.l_copies())
-        final = total(self.t.sum_x[...], self.t.got_l[...])
-        return jnp.where(self.n.yh == 1, pltpu.roll(final, 192, 1), final)
-
-
-def share_squares(n, final):
+        self.wait(self.third_copies())
+        return total(self.t.mid[...], *[self.t.got_y[i] for i in range(3)])
+
+
+def group_squares(n, final):
     matrix, other = final[0:48, :], final[48:80, :]
-    row = lax.broadcasted_iota(jnp.int32, (48, 256), 0)
-    lane = lax.broadcasted_iota(jnp.int32, (48, 256), 1)
-    low = 4 * n.x + 18 * n.yl
-    squares = jnp.sum(jnp.where((row >= low) & (row < low + 18) & (lane < C), matrix * matrix, 0.0), axis=0, keepdims=True)
-    row = lax.broadcasted_iota(jnp.int32, (32, 256), 0)
-    lane = lax.broadcasted_iota(jnp.int32, (32, 256), 1)
-    index = (row + x_row(n.b, n.z, n.x)) * WT + lane
-    low = 975 * (32 * n.b + n.j)
-    inside = (index >= low) & (index < low + 975) & (lane < WT)
-    squares = squares + jnp.sum(jnp.where(inside, other * other, 0.0), axis=0, keepdims=True)
+    row = lax.broadcasted_iota(jnp.int32, (48, 384), 0)
+    low = 4 * n.x
+    squares = jnp.sum(jnp.where((row >= low) & (row < low + 36), matrix * matrix, 0.0), axis=0, keepdims=True)
+    lane = lax.broadcasted_iota(jnp.int32, (32, 384), 1)
+    row = lax.broadcasted_iota(jnp.int32, (32, 384), 0) + x_row(n.core, n.z, n.x)
+    for yh in range(2):
+        lat = 2 * yh + n.core
+        at = lane - C * yh
+        index = (row + lat_row(lat)) * WT + at
+        low = 975 * (32 * lat + 8 * n.z + 2 * n.x)
+        inside = (index >= low) & (index < low + 1950) & (at >= 0) & (at < WT)
+        squares = squares + jnp.sum(jnp.where(inside, other * other, 0.0), axis=0, keepdims=True)
     return jnp.sum(squares, axis=1, keepdims=True)
+
+
+def own_lanes(n, final):
+    return jnp.where(n.yh == 1, pltpu.roll(final, C, 1), final)[:, 0:256]
 
 
 INPUTS = ["tok", "cot", "gains", "w_qkv", "w_proj", "w_up", "w_down", "bias", "to_win", "to_nat", "send_win", "win_send", "send_nat", "to_slots", "from_slots"]
@@ -502,17 +502,20 @@
 BLOCK = [
     ("x", (NT, C), BF), ("wq", (3, C, C), BF), ("q", (NT, C), BF), ("k", (NT, C), BF), ("v", (NT, C), BF), ("p", (4 * BROWS, WT), BF),
     ("mix", (NT, C), BF), ("hid", (NT, C), F32), ("a", (NT, FFN), BF), ("gp", (NT, FFN), BF), ("dout", (NT, C), BF), ("part", (2, 816, 384), BF),
-    ("got_core", (816, 384), BF), ("sum_core", (816, 384), BF), ("got_z", (3, 224, 384), BF), ("sum_z", (224, 384), BF),
-    ("got_y", (224, 256), BF), ("sum_y", (224, 256), BF), ("got_x", (3, 80, 256), BF), ("sum_x", (80, 256), BF), ("got_l", (80, 256), BF),
+    ("got_core", (816, 384), BF), ("sum_m", (4, 144, 384), BF), ("sum_o", (240, 384), BF),
+    ("got_x", (3, 4, 48, 256), BF), ("got_o", (3, 80, 384), BF), ("got_z", (3, 144, 128), BF),
+    ("sum_x", (4, 48, 256), BF), ("sum_zo", (80, 384), BF), ("sum_z", (144, 128), BF),
+    ("got_xz", (3, 48, 256), BF), ("got_ox", (3, 32, 384), BF), ("got_zx", (3, 48, 128), BF),
+    ("mid", (80, 384), BF), ("got_y", (3, 80, 384), BF),
     ("db", (OROWS, WT), F32), ("dg", (2, C), F32),
 ]
 SHARED = [
     ("out", (NT, C), BF), ("dx", (NT, C), BF), ("u", (NT, C), BF), ("n2", (NT, C), BF), ("datt", (NT, C), BF), ("dq", (NT, C), BF), ("dk", (NT, C), BF),
-    ("dv", (NT, C), BF), ("dup", (NT, FFN), BF), ("dom", (BROWS, C), BF), ("qm", (BROWS, C), BF), ("ds", (BROWS, WT), BF),
+    ("dv", (NT, C), BF), ("dup", (NT, FFN), BF),
     ("lbias", (3, BROWS, WT), F32), ("db_b", (BROWS, WT), F32), ("parts", (24, 8, 128), F32),
     ("cot_src", (NR, C), BF), ("cot_dst", (NR, C), BF), ("mid_src", (NR, C), BF), ("mid_dst", (NR, C), BF), ("back_src", (NR, C), BF), ("back_dst", (NR, C), BF),
 ]
-SEMS = 15 + 30 + 22
+SEMS = 15 + 44 + 16
 
 
 def place(nlat, nlon):
@@ -549,17 +552,15 @@
 
     plane = [(dz, dx) for dz in range(4) for dx in range(4) if (dz, dx) != (0, 0)]
     plane_dev = [n.device(z=(n.z + dz) % 4, x=(n.x + dx) % 4) for dz, dx in plane]
-    cube = [(a, c, e) for a in range(2) for c in range(2) for e in range(2) if (a, c, e) != (0, 0, 0)]
-    cube_dev = [n.device(yh=(n.yh + a) % 2, core=(n.core + c) % 2, yl=(n.yl + e) % 2) for a, c, e in cube]
-    far = plane_dev + cube_dev if reduce else []
+    pal = n.device(core=1 - n.core)
+    y_dev = [n.device(yl=1 - n.yl), n.device(yh=1 - n.yh), n.device(yl=1 - n.yl, yh=1 - n.yh)]
+    far = plane_dev + y_dev + [pal] if reduce else []
     greet(
         [(None, (n.b, n.east)), (None, (n.b, n.west)), (n.inner_up, (n.up, n.j)), (n.inner_down, (n.down, n.j)), (n.inner_up, (n.up, n.east)), (n.inner_down, (n.down, n.west))]
-        + [(None, d) for d in far],
-        jnp.where(jnp.logical_or(n.first, n.last), 4, 6) + len(far),
+        + [(None, d) for d in far]
     )
 
     one.cot_src[...] = shuffle(one.send_nat[...], one.cot[...])
-    ex_cot.start()
     one.x[...] = shuffle(one.to_win[...], one.tok[...])
     for b, t in enumerate(blocks):
         for i in range(3):
@@ -567,7 +568,9 @@
     one.lbias[0] = one.bias[0] * LOG2E
     forward_windows(one, 0, lambda w, h: one.lbias[0, h * WT:h * WT + WT, :], False)
     one.mid_src[...] = shuffle(one.send_win[...], one.out[...])
+    pl.semaphore_wait(pltpu.get_barrier_semaphore(), jnp.where(jnp.logical_or(n.first, n.last), 4, 6) + len(far))
     ex_mid.start()
+    ex_cot.start()
 
     for group in range(2):
         polar = n.first if group == 0 else n.last
@@ -584,8 +587,6 @@
 
     two.db[...] = jnp.zeros((OROWS, WT), F32)
     two.db_b[...] = jnp.zeros((BROWS, WT), F32)
-    ex_cot.finish()
-    two.dout[...] = shuffle(two.to_slots[...], two.cot_dst[...])
     ex_mid.finish()
     two.x[...] = shuffle(two.to_slots[...], two.mid_dst[...])
     forward_windows(two, 1, lambda w, h: two.lbias[1 + w // 2, h * WT:h * WT + WT, :], True)
@@ -601,6 +602,8 @@
         def _():
             two.db_b[rows, :] += ds
 
+    ex_cot.finish()
+    two.dout[...] = shuffle(two.to_slots[...], two.cot_dst[...])
     backward_windows(two, 1, dbias_two, lambda w: None)
     two.back_src[...] = shuffle(two.from_slots[...], two.dx[...])
     ex_back.start()
@@ -615,7 +618,7 @@
     weight_products(two, two.part)
     other_rows(two, two.part)
     red_one = Reduce(n, one, *sems, 15)
-    red_two = Reduce(n, two, *sems, 30)
+    red_two = Reduce(n, two, *sems, 37)
     if reduce:
         red_two.core_start()
 
@@ -628,9 +631,7 @@
 
     def step(w):
         if reduce:
-            pl.when(w == 0)(red_two.core_to_z)
-            pl.when(w == 2)(red_two.z_to_y)
-            pl.when(w == 3)(red_two.y_to_x)
+            pl.when(w == 1)(red_two.core_to_first)
 
     backward_windows(one, 0, dbias_one, step)
     weight_products(one, one.part)
@@ -640,16 +641,17 @@
     r["gtok"][...] = shuffle(one.to_nat[...], one.dx[...])
     if not reduce:
         return
-    red_two.x_to_l()
-    red_one.core_to_z()
+    red_two.first_to_second()
+    red_one.core_to_first()
+    red_two.second_to_third()
     two_final = red_two.finish()
-    red_one.z_to_y()
-    red_one.y_to_x()
-    red_one.x_to_l()
+    squares = group_squares(n, two_final)
+    red_one.first_to_second()
+    red_one.second_to_third()
     one_final = red_one.finish()
 
     parts = one.parts
-    parts[0] = jnp.broadcast_to(share_squares(n, one_final) + share_squares(n, two_final), (8, 128))
+    parts[0] = jnp.broadcast_to(squares + group_squares(n, one_final), (8, 128))
 
     def spread(base, source, target, devices):
         copies = [
@@ -665,11 +667,12 @@
             acc = acc + parts[target + i]
         return acc
 
-    parts[16] = spread(45, 0, 1, plane_dev)
-    acc = spread(60, 16, 17, cube_dev)
+    parts[16] = spread(59, 0, 1, plane_dev)
+    acc = spread(74, 16, 17, [pal])
     ceiling = math.sqrt(24 * C * C + 2 * VECB)
     factor = jnp.minimum(1.0, ceiling / (jnp.sqrt(acc) + 1e-06))[0:1, 0:1]
     for b, final in enumerate((one_final, two_final)):
+        final = own_lanes(n, final)
         r["m"][b] = final[0:48, :] * factor
         r["o"][b] = final[48:80, :] * factor
 
@@ -694,7 +697,7 @@
     n = place(nlat, nlon)
     m = lax.dynamic_slice_in_dim(m, 4 * n.x + 18 * n.yl, 18, axis=1)[:, :, :C]
     flat = o[:, :, :WT].reshape(2, 32 * WT)
-    other = lax.dynamic_slice_in_dim(flat, 975 * (32 * n.b + n.j) - x_row(n.b, n.z, n.x) * WT, 975, axis=1)
+    other = lax.dynamic_slice_in_dim(flat, 975 * (32 * n.b + n.j) - (lat_row(n.b) + x_row(n.core, n.z, n.x)) * WT, 975, axis=1)
     return gtok.reshape(tokens.shape), m.transpose(0, 2, 1), other
 
 

time: 112 us -> 86.5 us (0.77)
  Pallas kernels: 106 us -> 80.7 us
    pallas_call x1, Pallas kernels: 106 us -> 80.7 us  [run(): pl.pallas_call(functools.partial(kernel, nlat, nlon, reduce), in_specs=[v...]
where the time goes in v3:
time: 86.5 us; the launch traced here: 86.3 us
  Pallas kernels  80.7 us (93%)
  local copies, waits for them, and re-layouts  4.82 us (6%)
    pallas_call x1, Pallas kernels, run(): pl.pallas_call(functools.partial(kernel, nlat, nlon, reduce), in_specs=[v...  80.7 us
    unnamed x2, local copies, waits for them, and re-layouts  2.33 us

profile of v3, /device:TPU:1, one launch (start us, length us, event | category | flops | bytes accessed | tf_op | source)
XLA Modules:
  0.0 86.3 jit_solution(2755459279959542091)
XLA Ops:
  0.7 80.7 %two_blocks.1 = (bf16[576,192]{1,0:T(8,128)(2,1)}, f32[2,48,256]{2,1,0:T(8,128)}, f32[2,32,256]{2,1,0:T(8,128)}) custom-call(bf16[576,192]{1,0:T(8,128)(2,1)} %bitcast.10, bf16[576,192]{1,0:T(8,128)(2,1)} %bitcast.11, f32[2,2,192]{2,1,0:T(2,128)} %refs_2_.1, bf16[2,192,576]{2,1,0:T(8,128)(2,1)} %refs_3_.1, bf16[2,192,192]{2,1,0:T(8,128)(2,1)} %refs_4_.1, ...), custom_call_target="tpu_custom_call" | custom-call | tf_op jit(solution)/shard_map/two_blocks/pallas_call | solution.py:684
  81.4 1.0 %reshape.25 = f32[2,4608]{1,0:T(2,128)S(1)} reshape(f32[2,32,144]{2,1,0:T(8,128)} %bitcast.13) | data formatting | bytes 73728 | tf_op jit(solution)/shard_map/reshape | solution.py:699
  82.4 0.7 constant_dynamic-slice_fusion
  83.1 0.8 dynamic-slice_bitcast_fusion
  83.9 0.6 copy.18
  84.6 1.7 %copy.20 = bf16[2,6,48,192]{3,2,1,0:T(8,128)(2,1)} copy(bf16[2,6,48,192]{3,2,1,0:T(8,128)(2,1)} %bitcast.12) | data formatting | bytes 442368

commit v4 on v3

--- a/solution.py
+++ b/solution.py
@@ -498,7 +498,12 @@
 
 INPUTS = ["tok", "cot", "gains", "w_qkv", "w_proj", "w_up", "w_down", "bias", "to_win", "to_nat", "send_win", "win_send", "send_nat", "to_slots", "from_slots"]
 PERMS = INPUTS[8:]
-OUTPUTS = [("gtok", (NT, C), BF), ("m", (2, 48, 256), F32), ("o", (2, 32, 256), F32)]
+OUTPUTS = [("gtok", (NT, C), BF), ("m", (18, 2, C), F32), ("o", (2, 975), F32)]
+COPIED = ["to_win", "tok", "w_qkv", "bias", "w_proj", "w_up", "w_down", "send_win", "send_nat", "cot", "to_slots", "from_slots", "win_send", "to_nat"]
+SHAPES = {
+    "tok": (NT, C), "cot": (NT, C), "w_qkv": (2, C, 3 * C), "w_proj": (2, C, C), "w_up": (2, C, FFN), "w_down": (2, C, FFN), "bias": (2, BROWS, WT),
+    "to_win": (NT, NT), "to_nat": (NT, NT), "send_win": (NR, NT), "win_send": (NT, NR), "send_nat": (NR, NT), "to_slots": (NT, NR), "from_slots": (NR, NT),
+}
 BLOCK = [
     ("x", (NT, C), BF), ("wq", (3, C, C), BF), ("q", (NT, C), BF), ("k", (NT, C), BF), ("v", (NT, C), BF), ("p", (4 * BROWS, WT), BF),
     ("mix", (NT, C), BF), ("hid", (NT, C), F32), ("a", (NT, FFN), BF), ("gp", (NT, FFN), BF), ("dout", (NT, C), BF), ("part", (2, 816, 384), BF),
@@ -512,7 +517,7 @@
 SHARED = [
     ("out", (NT, C), BF), ("dx", (NT, C), BF), ("u", (NT, C), BF), ("n2", (NT, C), BF), ("datt", (NT, C), BF), ("dq", (NT, C), BF), ("dk", (NT, C), BF),
     ("dv", (NT, C), BF), ("dup", (NT, FFN), BF),
-    ("lbias", (3, BROWS, WT), F32), ("db_b", (BROWS, WT), F32), ("parts", (24, 8, 128), F32),
+    ("lbias", (3, BROWS, WT), F32), ("db_b", (BROWS, WT), F32), ("parts", (24, 8, 128), F32), ("own", (2, 80, 256), F32),
     ("cot_src", (NR, C), BF), ("cot_dst", (NR, C), BF), ("mid_src", (NR, C), BF), ("mid_dst", (NR, C), BF), ("back_src", (NR, C), BF), ("back_dst", (NR, C), BF),
 ]
 SEMS = 15 + 44 + 16
@@ -536,9 +541,17 @@
 
 
 def kernel(nlat, nlon, reduce, *refs):
-    names = INPUTS + [o[0] for o in OUTPUTS] + ["first_" + e[0] for e in BLOCK] + ["second_" + e[0] for e in BLOCK] + [e[0] for e in SHARED] + ["send_sem", "recv_sem"]
+    names = INPUTS + [o[0] for o in OUTPUTS] + ["first_" + e[0] for e in BLOCK] + ["second_" + e[0] for e in BLOCK] + [e[0] for e in SHARED] + ["in_" + k for k in COPIED] + ["send_sem", "recv_sem", "in_sem"]
     r = dict(zip(names, refs, strict=True))
-    weights = {k: r[k] for k in INPUTS}
+    loads = {k: pltpu.make_async_copy(r[k], r["in_" + k], r["in_sem"].at[i]) for i, k in enumerate(COPIED)}
+    for copy in loads.values():
+        copy.start()
+
+    def need(*keys):
+        for k in keys:
+            loads[k].wait()
+
+    weights = {k: r["in_" + k] if k in COPIED else r[k] for k in INPUTS}
     blocks = []
     for label in ("first_", "second_"):
         blocks.append(types.SimpleNamespace(**weights, **{e[0]: r[e[0]] for e in SHARED}, **{e[0]: r[label + e[0]] for e in BLOCK}))
@@ -560,17 +573,24 @@
         + [(None, d) for d in far]
     )
 
-    one.cot_src[...] = shuffle(one.send_nat[...], one.cot[...])
+    need("to_win", "tok")
     one.x[...] = shuffle(one.to_win[...], one.tok[...])
+    need("w_qkv")
     for b, t in enumerate(blocks):
         for i in range(3):
             t.wq[i] = t.w_qkv[b, :, C * i:C * i + C]
+    need("bias")
     one.lbias[0] = one.bias[0] * LOG2E
+    need("w_proj", "w_up", "w_down")
     forward_windows(one, 0, lambda w, h: one.lbias[0, h * WT:h * WT + WT, :], False)
+    need("send_win")
     one.mid_src[...] = shuffle(one.send_win[...], one.out[...])
     pl.semaphore_wait(pltpu.get_barrier_semaphore(), jnp.where(jnp.logical_or(n.first, n.last), 4, 6) + len(far))
     ex_mid.start()
+    need("send_nat", "cot")
+    one.cot_src[...] = shuffle(one.send_nat[...], one.cot[...])
     ex_cot.start()
+    need("to_slots", "from_slots", "win_send", "to_nat")
 
     for group in range(2):
         polar = n.first if group == 0 else n.last
@@ -671,22 +691,30 @@
     acc = spread(74, 16, 17, [pal])
     ceiling = math.sqrt(24 * C * C + 2 * VECB)
     factor = jnp.minimum(1.0, ceiling / (jnp.sqrt(acc) + 1e-06))[0:1, 0:1]
+    first_row = 4 * n.x + 18 * n.yl
+    start = 975 * (32 * n.b + n.j) - (lat_row(n.b) + x_row(n.core, n.z, n.x)) * WT
+    rows = []
     for b, final in enumerate((one_final, two_final)):
-        final = own_lanes(n, final)
-        r["m"][b] = final[0:48, :] * factor
-        r["o"][b] = final[48:80, :] * factor
+        one.own[b] = own_lanes(n, final) * factor
+        for i in range(18):
+            r["m"][i, b:b + 1, :] = one.own[b, pl.ds(first_row + i, 1), 0:C]
+        rows.append(jnp.concatenate([one.own[b, pl.ds(48 + start // WT + i, 1), 0:WT] for i in range(8)], axis=1))
+    flat = jnp.concatenate(rows + [jnp.zeros((6, 8 * WT), F32)], axis=0)
+    r["o"][...] = pltpu.roll(flat, 8 * WT - start % WT, 1)[0:2, 0:975]
 
 
 def run(nlat, nlon, reduce, tokens, cotangent, norm_gains, w_qkv, w_proj, w_up, w_down, pos_bias):
     args = [tokens.reshape(NT, C), cotangent.reshape(NT, C), norm_gains, w_qkv, w_proj, w_up, jnp.swapaxes(w_down, 1, 2), pos_bias.reshape(2, BROWS, WT)]
     args += [const(p) for p in PERMS]
     vmem = pl.BlockSpec(memory_space=pltpu.VMEM)
+    anywhere = pl.BlockSpec(memory_space=pl.ANY)
     return pl.pallas_call(
         functools.partial(kernel, nlat, nlon, reduce),
-        in_specs=[vmem] * len(args),
+        in_specs=[anywhere if k in COPIED else vmem for k in INPUTS],
         out_specs=[vmem] * len(OUTPUTS),
         out_shape=[jax.ShapeDtypeStruct(s, d) for _, s, d in OUTPUTS],
-        scratch_shapes=[pltpu.VMEM(s, d) for _, s, d in BLOCK + BLOCK + SHARED] + [pltpu.SemaphoreType.DMA((SEMS,))] * 2,
+        scratch_shapes=[pltpu.VMEM(s, d) for _, s, d in BLOCK + BLOCK + SHARED] + [pltpu.VMEM(SHAPES[k], F32 if k == "bias" else BF) for k in COPIED]
+        + [pltpu.SemaphoreType.DMA((SEMS,))] * 2 + [pltpu.SemaphoreType.DMA((len(COPIED),))],
         compiler_params=pltpu.CompilerParams(vmem_limit_bytes=VMEM_LIMIT, collective_id=1, has_side_effects=True),
         name="two_blocks",
     )(*args)
@@ -694,11 +722,7 @@
 
 def shards(nlat, nlon, tokens, *args):
     gtok, m, o = run(nlat, nlon, True, tokens, *args)
-    n = place(nlat, nlon)
-    m = lax.dynamic_slice_in_dim(m, 4 * n.x + 18 * n.yl, 18, axis=1)[:, :, :C]
-    flat = o[:, :, :WT].reshape(2, 32 * WT)
-    other = lax.dynamic_slice_in_dim(flat, 975 * (32 * n.b + n.j) - (lat_row(n.b) + x_row(n.core, n.z, n.x)) * WT, 975, axis=1)
-    return gtok.reshape(tokens.shape), m.transpose(0, 2, 1), other
+    return gtok.reshape(tokens.shape), m.transpose(1, 2, 0), o
 
 
 def solution(mesh):

time: 86.5 us -> 85.2 us (0.985)
    unnamed x2 -> x3, local copies, waits for them, and re-layouts: 2.33 us -> 4.38 us
    reshape x1 -> x0, local copies, waits for them, and re-layouts: 0.96 us -> none  [shards(): flat = o[:, :, :WT].reshape(2, 32 * WT)]
where the time goes in v4:
time: 85.2 us; the launch traced here: 84.9 us
  Pallas kernels  79.9 us (94%)
  local copies, waits for them, and re-layouts  4.38 us (5%)
    pallas_call x1, Pallas kernels, run(): pl.pallas_call(functools.partial(kernel, nlat, nlon, reduce), in_specs=[a...  79.9 us
    unnamed x3, local copies, waits for them, and re-layouts  4.38 us

profile of v4, /device:TPU:1, one launch (start us, length us, event | category | flops | bytes accessed | tf_op | source)
XLA Modules:
  0.0 84.9 jit_solution(5454345400522708674)
XLA Ops:
  0.6 79.9 %two_blocks.1 = (bf16[576,192]{1,0:T(8,128)(2,1)}, f32[18,2,192]{2,1,0:T(2,128)}, f32[2,975]{1,0:T(2,128)}) custom-call(bf16[576,192]{1,0:T(8,128)(2,1)} %bitcast.8, bf16[576,192]{1,0:T(8,128)(2,1)} %bitcast.9, f32[2,2,192]{2,1,0:T(2,128)} %refs_2_.1, bf16[2,192,576]{2,1,0:T(8,128)(2,1)} %refs_3_.1, bf16[2,192,192]{2,1,0:T(8,128)(2,1)} %refs_4_.1, ...), custom_call_target="tpu_custom_call" | custom-call | tf_op jit(solution)/shard_map/two_blocks/pallas_call | solution.py:711
  80.5 1.7 %copy.21 = bf16[2,6,48,192]{3,2,1,0:T(8,128)(2,1)} copy(bf16[2,6,48,192]{3,2,1,0:T(8,128)(2,1)} %bitcast.10) | data formatting | bytes 442368
  82.2 1.4 %copy.22 = f32[2,192,18]{1,0,2:T(2,128)} copy(f32[2,192,18]{1,0,2:T(2,128)} %bitcast.11) | data formatting | bytes 55296
  83.6 1.3 %copy.23 = f32[2,975]{1,0:T(2,128)} copy(f32[2,975]{1,0:T(2,128)} %get-tuple-element.14) | data formatting | bytes 15600

commit v5 on v4

--- a/solution.py
+++ b/solution.py
@@ -167,7 +167,7 @@
     lax.fori_loop(0, 4, window, 0, unroll=2)
 
 
-def backward_windows(t, b, dbias_of, after_window):
+def backward_windows(t, b, dbias_of):
     g0, g1 = t.gains[b, 0:1, :], t.gains[b, 1:2, :]
     t.dg[...] = jnp.zeros((2, C), F32)
 
@@ -222,7 +222,6 @@
         t.dg[0:1, :] += jnp.sum(du * xhat, axis=0, keepdims=True)
         dx = norm_back(du, g0, xhat, r).astype(BF).astype(F32) + datt.astype(F32)
         t.dx[rows, :] = dx.astype(BF)
-        after_window(w)
         return carry
 
     lax.fori_loop(0, 4, window, 0, unroll=2)
@@ -517,10 +516,10 @@
 SHARED = [
     ("out", (NT, C), BF), ("dx", (NT, C), BF), ("u", (NT, C), BF), ("n2", (NT, C), BF), ("datt", (NT, C), BF), ("dq", (NT, C), BF), ("dk", (NT, C), BF),
     ("dv", (NT, C), BF), ("dup", (NT, FFN), BF),
-    ("lbias", (3, BROWS, WT), F32), ("db_b", (BROWS, WT), F32), ("parts", (24, 8, 128), F32), ("own", (2, 80, 256), F32),
-    ("cot_src", (NR, C), BF), ("cot_dst", (NR, C), BF), ("mid_src", (NR, C), BF), ("mid_dst", (NR, C), BF), ("back_src", (NR, C), BF), ("back_dst", (NR, C), BF),
+    ("lbias", (3, BROWS, WT), F32), ("db_pair", (2, BROWS, WT), F32), ("parts", (32, 1, 128), F32), ("own", (2, 80, 256), F32),
+    ("cot_src", (NR, 256), BF), ("cot_dst", (NR, 256), BF), ("mid_src", (NR, 256), BF), ("mid_dst", (NR, 256), BF), ("back_src", (NR, 256), BF), ("back_dst", (NR, 256), BF),
 ]
-SEMS = 15 + 44 + 16
+SEMS = 15 + 44 + 31
 
 
 def place(nlat, nlon):
@@ -563,11 +562,10 @@
     ex_mid = Exchange(moves_out(n), one.mid_src, one.mid_dst, *sems, 5, here)
     ex_back = Exchange(moves_back(n), one.back_src, one.back_dst, *sems, 10, here)
 
-    plane = [(dz, dx) for dz in range(4) for dx in range(4) if (dz, dx) != (0, 0)]
-    plane_dev = [n.device(z=(n.z + dz) % 4, x=(n.x + dx) % 4) for dz, dx in plane]
-    pal = n.device(core=1 - n.core)
+    level = [(e, dz, dx) for e in range(2) for dz in range(4) for dx in range(4) if (e, dz, dx) != (0, 0, 0)]
+    level_dev = [n.device(core=(n.core + e) % 2, z=(n.z + dz) % 4, x=(n.x + dx) % 4) for e, dz, dx in level]
     y_dev = [n.device(yl=1 - n.yl), n.device(yh=1 - n.yh), n.device(yl=1 - n.yl, yh=1 - n.yh)]
-    far = plane_dev + y_dev + [pal] if reduce else []
+    far = level_dev + y_dev if reduce else []
     greet(
         [(None, (n.b, n.east)), (None, (n.b, n.west)), (n.inner_up, (n.up, n.j)), (n.inner_down, (n.down, n.j)), (n.inner_up, (n.up, n.east)), (n.inner_down, (n.down, n.west))]
         + [(None, d) for d in far]
@@ -584,11 +582,11 @@
     need("w_proj", "w_up", "w_down")
     forward_windows(one, 0, lambda w, h: one.lbias[0, h * WT:h * WT + WT, :], False)
     need("send_win")
-    one.mid_src[...] = shuffle(one.send_win[...], one.out[...])
+    one.mid_src[:, 0:C] = shuffle(one.send_win[...], one.out[...])
     pl.semaphore_wait(pltpu.get_barrier_semaphore(), jnp.where(jnp.logical_or(n.first, n.last), 4, 6) + len(far))
     ex_mid.start()
     need("send_nat", "cot")
-    one.cot_src[...] = shuffle(one.send_nat[...], one.cot[...])
+    one.cot_src[:, 0:C] = shuffle(one.send_nat[...], one.cot[...])
     ex_cot.start()
     need("to_slots", "from_slots", "win_send", "to_nat")
 
@@ -605,36 +603,27 @@
         def _():
             two.lbias[1 + group] = two.bias[1] * LOG2E
 
-    two.db[...] = jnp.zeros((OROWS, WT), F32)
-    two.db_b[...] = jnp.zeros((BROWS, WT), F32)
+    two.db_pair[...] = jnp.zeros((2, BROWS, WT), F32)
     ex_mid.finish()
-    two.x[...] = shuffle(two.to_slots[...], two.mid_dst[...])
+    two.x[...] = shuffle(two.to_slots[...], two.mid_dst[:, 0:C])
     forward_windows(two, 1, lambda w, h: two.lbias[1 + w // 2, h * WT:h * WT + WT, :], True)
 
     def dbias_two(w, h, ds):
-        rows = slice(h * WT, h * WT + WT)
-
-        @pl.when(w < 2)
-        def _():
-            two.db[rows, :] += ds
-
-        @pl.when(w >= 2)
-        def _():
-            two.db_b[rows, :] += ds
+        two.db_pair[w // 2, h * WT:h * WT + WT, :] += ds
 
     ex_cot.finish()
-    two.dout[...] = shuffle(two.to_slots[...], two.cot_dst[...])
-    backward_windows(two, 1, dbias_two, lambda w: None)
-    two.back_src[...] = shuffle(two.from_slots[...], two.dx[...])
+    two.dout[...] = shuffle(two.to_slots[...], two.cot_dst[:, 0:C])
+    backward_windows(two, 1, dbias_two)
+    two.back_src[:, 0:C] = shuffle(two.from_slots[...], two.dx[...])
     ex_back.start()
-    for group, ref in enumerate((two.db, two.db_b)):
+    for group in range(2):
         @pl.when(n.first if group == 0 else n.last)
         def _():
             for h in range(HEADS):
                 rows = slice(h * WT, h * WT + WT)
-                ref[rows, :] = polar_back(ref[rows, :], group == 1)
-
-    two.db[0:BROWS, :] += two.db_b[...]
+                two.db_pair[group, rows, :] = polar_back(two.db_pair[group, rows, :], group == 1)
+
+    two.db[0:BROWS, :] = two.db_pair[0] + two.db_pair[1]
     weight_products(two, two.part)
     other_rows(two, two.part)
     red_one = Reduce(n, one, *sems, 15)
@@ -643,17 +632,15 @@
         red_two.core_start()
 
     ex_back.finish()
-    one.dout[...] = shuffle(one.win_send[...], one.back_dst[...])
+    if reduce:
+        red_two.core_to_first()
+    one.dout[...] = shuffle(one.win_send[...], one.back_dst[:, 0:C])
     one.db[...] = jnp.zeros((OROWS, WT), F32)
 
     def dbias_one(w, h, ds):
         one.db[h * WT:h * WT + WT, :] += ds
 
-    def step(w):
-        if reduce:
-            pl.when(w == 1)(red_two.core_to_first)
-
-    backward_windows(one, 0, dbias_one, step)
+    backward_windows(one, 0, dbias_one)
     weight_products(one, one.part)
     other_rows(one, one.part)
     if reduce:
@@ -671,24 +658,18 @@
     one_final = red_one.finish()
 
     parts = one.parts
-    parts[0] = jnp.broadcast_to(squares + group_squares(n, one_final), (8, 128))
-
-    def spread(base, source, target, devices):
-        copies = [
-            pltpu.make_async_remote_copy(src_ref=parts.at[source], dst_ref=parts.at[target + i], send_sem=sems[0].at[base + i], recv_sem=sems[1].at[base + i], device_id=d, device_id_type=MESH)
-            for i, d in enumerate(devices)
-        ]
-        for c in copies:
-            c.start()
-        for c in copies:
-            c.wait()
-        acc = parts[source]
-        for i in range(len(devices)):
-            acc = acc + parts[target + i]
-        return acc
-
-    parts[16] = spread(59, 0, 1, plane_dev)
-    acc = spread(74, 16, 17, [pal])
+    parts[0] = jnp.broadcast_to(squares + group_squares(n, one_final), (1, 128))
+    copies = [
+        pltpu.make_async_remote_copy(src_ref=parts.at[0], dst_ref=parts.at[1 + i], send_sem=sems[0].at[59 + i], recv_sem=sems[1].at[59 + i], device_id=d, device_id_type=MESH)
+        for i, d in enumerate(level_dev)
+    ]
+    for c in copies:
+        c.start()
+    for c in copies:
+        c.wait()
+    acc = parts[0]
+    for i in range(len(copies)):
+        acc = acc + parts[1 + i]
     ceiling = math.sqrt(24 * C * C + 2 * VECB)
     factor = jnp.minimum(1.0, ceiling / (jnp.sqrt(acc) + 1e-06))[0:1, 0:1]
     first_row = 4 * n.x + 18 * n.yl
@@ -720,8 +701,29 @@
     )(*args)
 
 
+def copy_out(*refs):
+    half = len(OUTPUTS)
+    copies = [pltpu.make_async_copy(refs[i], refs[half + i], refs[2 * half].at[i]) for i in range(half)]
+    for c in copies:
+        c.start()
+    for c in copies:
+        c.wait()
+
+
+def run_copy_out(results):
+    anywhere = pl.BlockSpec(memory_space=pl.ANY)
+    return pl.pallas_call(
+        copy_out,
+        in_specs=[anywhere] * len(results),
+        out_specs=[anywhere] * len(results),
+        out_shape=[jax.ShapeDtypeStruct(s, d) for _, s, d in OUTPUTS],
+        scratch_shapes=[pltpu.SemaphoreType.DMA((len(OUTPUTS),))],
+        name="copy_out",
+    )(*results)
+
+
 def shards(nlat, nlon, tokens, *args):
-    gtok, m, o = run(nlat, nlon, True, tokens, *args)
+    gtok, m, o = run_copy_out(run(nlat, nlon, True, tokens, *args))
     return gtok.reshape(tokens.shape), m.transpose(1, 2, 0), o
 
 

time: 85.2 us -> 89.1 us (1.046)
  Pallas kernels: 79.9 us -> 88.2 us
  local copies, waits for them, and re-layouts: 4.38 us -> 0 us
    pallas_call x0 -> x1, Pallas kernels: none -> 11.4 us  [run_copy_out(): pl.pallas_call(copy_out, in_specs=[anywhere] * len(results), out_specs=[a...]
    unnamed x3 -> x0, local copies, waits for them, and re-layouts: 4.38 us -> none
    pallas_call x1, Pallas kernels: 79.9 us -> 76.7 us  [run(): pl.pallas_call(functools.partial(kernel, nlat, nlon, reduce), in_specs=[a...]
where the time goes in v5:
time: 89.1 us; the launch traced here: 89 us
  Pallas kernels  88.2 us (99%)
    pallas_call x1, Pallas kernels, run(): pl.pallas_call(functools.partial(kernel, nlat, nlon, reduce), in_specs=[a...  76.7 us
    pallas_call x1, Pallas kernels, run_copy_out(): pl.pallas_call(copy_out, in_specs=[anywhere] * len(results), out_specs=[a...  11.4 us

profile of v5, /device:TPU:1, one launch (start us, length us, event | category | flops | bytes accessed | tf_op | source)
XLA Modules:
  0.0 89.0 jit_solution(7963146883464465791)
XLA Ops:
  0.6 76.7 %two_blocks.1 = (bf16[576,192]{1,0:T(8,128)(2,1)}, f32[18,2,192]{2,1,0:T(2,128)}, f32[2,975]{1,0:T(2,128)}) custom-call(bf16[576,192]{1,0:T(8,128)(2,1)} %bitcast.8, bf16[576,192]{1,0:T(8,128)(2,1)} %bitcast.9, f32[2,2,192]{2,1,0:T(2,128)} %refs_2_.1, bf16[2,192,576]{2,1,0:T(8,128)(2,1)} %refs_3_.1, bf16[2,192,192]{2,1,0:T(8,128)(2,1)} %refs_4_.1, ...), custom_call_target="tpu_custom_call" | custom-call | tf_op jit(solution)/shard_map/two_blocks/pallas_call | solution.py:692
  77.4 11.4 %copy_out.1 = (bf16[576,192]{1,0:T(8,128)(2,1)}, f32[18,2,192]{2,1,0:T(2,128)}, f32[2,975]{1,0:T(2,128)}) custom-call(bf16[576,192]{1,0:T(8,128)(2,1)} %get-tuple-element.9.refs_0_, f32[18,2,192]{2,1,0:T(2,128)} %get-tuple-element.10.refs_1_, f32[2,975]{1,0:T(2,128)} %get-tuple-element.11.refs_2_), custom_call_target="tpu_custom_call" | custom-call | tf_op jit(solution)/shard_map/copy_out/pallas_call | solution.py:715

commit v6 on v5

--- a/solution.py
+++ b/solution.py
@@ -167,11 +167,22 @@
     lax.fori_loop(0, 4, window, 0, unroll=2)
 
 
-def backward_windows(t, b, dbias_of):
-    g0, g1 = t.gains[b, 0:1, :], t.gains[b, 1:2, :]
+def pairs(window, after_first=None):
+    def body(i, carry):
+        window(2 * i)
+        window(2 * i + 1)
+        if after_first is not None:
+            pl.when(i == 0)(after_first)
+        return carry
+
+    lax.fori_loop(0, 2, body, 0)
+
+
+def backward_feed(t, b):
+    g1 = t.gains[b, 1:2, :]
     t.dg[...] = jnp.zeros((2, C), F32)
 
-    def window(w, carry):
+    def window(w):
         rows = pl.ds(pl.multiple_of(w * WT, WT), WT)
         dy = t.dout[rows, :]
         dn2 = jnp.zeros((WT, C), F32)
@@ -185,9 +196,17 @@
         xhat, r = stats(t.hid[rows, :])
         t.n2[rows, :] = (xhat * g1).astype(BF)
         t.dg[1:2, :] += jnp.sum(dn2 * xhat, axis=0, keepdims=True)
-        dhid = dy.astype(F32) + norm_back(dn2, g1, xhat, r)
-        datt = dhid.astype(BF)
-        t.datt[rows, :] = datt
+        t.datt[rows, :] = (dy.astype(F32) + norm_back(dn2, g1, xhat, r)).astype(BF)
+
+    pairs(window)
+
+
+def backward_attention(t, b, dbias_of, after_first):
+    g0 = t.gains[b, 0:1, :]
+
+    def window(w):
+        rows = pl.ds(pl.multiple_of(w * WT, WT), WT)
+        datt = t.datt[rows, :]
         dmix = nt(datt, t.w_proj[b]).astype(BF)
         q = t.q[rows, :]
         k = t.k[rows, :]
@@ -222,47 +241,51 @@
         t.dg[0:1, :] += jnp.sum(du * xhat, axis=0, keepdims=True)
         dx = norm_back(du, g0, xhat, r).astype(BF).astype(F32) + datt.astype(F32)
         t.dx[rows, :] = dx.astype(BF)
-        return carry
-
-    lax.fori_loop(0, 4, window, 0, unroll=2)
-
-
-def weight_products(t, part):
-    pad = jnp.zeros((NT, 64), BF)
-
-    def left(lhs, x):
-        return tn(lhs, jnp.concatenate([x, pad], axis=1))
-
-    def right(lhs, x):
-        return tn(lhs, jnp.concatenate([pad, x], axis=1))
-
-    def put(core, row, lft, rgt):
-        rows = slice(row, row + lft.shape[0])
-        part[core, rows, 0:128] = lft[:, 0:128].astype(BF)
-        part[core, rows, 128:256] = (lft[:, 128:256] + rgt[:, 0:128]).astype(BF)
-        part[core, rows, 256:384] = rgt[:, 128:256].astype(BF)
-
-    u, n2, dout = t.u[...], t.n2[...], t.dout[...]
-    up_low = left(t.dup[:, 0:384], n2)
-    up_high = right(t.dup[:, 384:768], n2)
-    put(0, 0, left(t.dq[...], u), up_high[0:192])
-    put(0, 192, left(t.dk[...], u), up_high[192:384])
-    down = right(t.a[:, 0:384], dout)
-    put(0, 384, left(t.dv[...], u), down[0:192])
-    put(1, 0, left(t.datt[...], t.mix[...]), down[192:384])
-    down = right(t.a[:, 384:768], dout)
-    put(1, 192, up_low[0:192], down[0:192])
-    put(1, 384, up_low[192:384], down[192:384])
-
-
-def other_rows(t, part):
+
+    pairs(window, after_first)
+
+
+def product_left(lhs, x):
+    return tn(lhs, jnp.concatenate([x, jnp.zeros((NT, 64), BF)], axis=1))
+
+
+def product_right(lhs, x):
+    return tn(lhs, jnp.concatenate([jnp.zeros((NT, 64), BF), x], axis=1))
+
+
+def products_early(t):
+    n2, dout = t.n2[...], t.dout[...]
+    down_low = product_right(t.a[:, 0:384], dout)
+    up_high = product_right(t.dup[:, 384:768], n2)
+    for i, right in enumerate((up_high[0:192], up_high[192:384], down_low[0:192])):
+        t.part[0, 192 * i:192 * i + 192, 128:384] = right.astype(BF)
+    down_high = product_right(t.a[:, 384:768], dout)
+    up_low = product_left(t.dup[:, 0:384], n2)
+    proj = product_left(t.datt[...], t.mix[...])
+    for i, (left, right) in enumerate(((proj, down_low[192:384]), (up_low[0:192], down_high[0:192]), (up_low[192:384], down_high[192:384]))):
+        rows = slice(192 * i, 192 * i + 192)
+        t.part[1, rows, 0:128] = left[:, 0:128].astype(BF)
+        t.part[1, rows, 128:256] = (left[:, 128:256] + right[:, 0:128]).astype(BF)
+        t.part[1, rows, 256:384] = right[:, 128:256].astype(BF)
+
+
+def products_late(t):
+    u = t.u[...]
+    for i, ref in enumerate((t.dq, t.dk, t.dv)):
+        rows = slice(192 * i, 192 * i + 192)
+        left = product_left(ref[...], u)
+        t.part[0, rows, 0:128] = left[:, 0:128].astype(BF)
+        t.part[0, rows, 128:256] = (left[:, 128:256] + t.part[0, rows, 128:256].astype(F32)).astype(BF)
+
+
+def other_rows(t):
     flat = jnp.concatenate([t.dg[0:1, :], t.dg[1:2, :], jnp.zeros((1, 3 * WT - 2 * C), F32)], axis=1)
     t.db[BROWS:OROWS, :] = jnp.concatenate([flat[:, 0:WT], flat[:, WT:2 * WT], flat[:, 2 * WT:3 * WT], jnp.zeros((OROWS - BROWS - 3, WT), F32)], axis=0)
     gap = jnp.zeros((240, 48), F32)
     for core in range(2):
         lft = t.db[lat_row(core):lat_row(core) + 240, :]
         rgt = t.db[lat_row(2 + core):lat_row(2 + core) + 240, :]
-        part[core, 576:816, :] = jnp.concatenate([lft, gap, rgt, gap], axis=1).astype(BF)
+        t.part[core, 576:816, :] = jnp.concatenate([lft, gap, rgt, gap], axis=1).astype(BF)
 
 
 def half_of(shape, axis):
@@ -397,20 +420,28 @@
 
     def core_copies(self):
         n, t = self.n, self.t
-        return [self.remote(0, t.part.at[1 - n.core], t.got_core, n.device(core=1 - n.core))]
+        pal = n.device(core=1 - n.core)
+        return (
+            self.remote(0, t.part.at[1, pl.ds(0, 576), :], t.got_core.at[pl.ds(0, 576), :], pal),
+            self.remote(1, t.part.at[0, pl.ds(0, 576), pl.ds(256, 128)], t.got_core.at[pl.ds(0, 576), pl.ds(256, 128)], pal),
+            self.remote(2, t.part.at[1 - n.core, pl.ds(576, 240), :], t.got_core.at[pl.ds(576, 240), :], pal),
+            self.remote(3, t.part.at[0, pl.ds(0, 576), pl.ds(0, 256)], t.got_core.at[pl.ds(0, 576), pl.ds(0, 256)], pal),
+        )
 
     def first_copies(self):
         n, t = self.n, self.t
-        out = []
+        tile2, tiles01, other = [], [], []
         for d in range(1, 4):
-            i = 3 * d - 2
+            i = 4 * d
             z = (n.z + d) % 4
             x = (n.x + d) % 4
-            out.append(self.remote(i, t.sum_m.at[:, pl.ds(al(32 * x), 48), pl.ds(128, 256)], t.got_x.at[d - 1], n.device(x=x)))
-            dev = n.device(z=z)
-            out.append(self.remote(i + 1, t.sum_o.at[pl.ds(al(z_row(n.core, z)), 80), :], t.got_o.at[d - 1], dev))
-            out.append(self.remote(i + 2, t.sum_m.at[z, :, pl.ds(0, 128)], t.got_z.at[d - 1], dev))
-        return out
+            to_x, to_z = n.device(x=x), n.device(z=z)
+            rows = pl.ds(al(32 * x), 48)
+            tile2.append(self.remote(i, t.sum_m.at[:, rows, pl.ds(256, 128)], t.got_x.at[d - 1, :, :, pl.ds(128, 128)], to_x))
+            tiles01.append(self.remote(i + 1, t.sum_m.at[:, rows, pl.ds(128, 128)], t.got_x.at[d - 1, :, :, pl.ds(0, 128)], to_x))
+            tiles01.append(self.remote(i + 2, t.sum_m.at[z, :, pl.ds(0, 128)], t.got_z.at[d - 1], to_z))
+            other.append(self.remote(i + 3, t.sum_o.at[pl.ds(al(z_row(n.core, z)), 80), :], t.got_o.at[d - 1], to_z))
+        return tile2, tiles01, other
 
     def x_window(self, x):
         return al(x_row(self.n.core, self.n.z, x) - z_row(self.n.core, self.n.z))
@@ -419,7 +450,7 @@
         n, t = self.n, self.t
         out = []
         for d in range(1, 4):
-            i = 3 * d + 7
+            i = 3 * d + 13
             z = (n.z + d) % 4
             x = (n.x + d) % 4
             out.append(self.remote(i, t.sum_x.at[z], t.got_xz.at[d - 1], n.device(z=z)))
@@ -431,7 +462,7 @@
     def third_copies(self):
         n, t = self.n, self.t
         devices = [n.device(yl=1 - n.yl), n.device(yh=1 - n.yh), n.device(yl=1 - n.yl, yh=1 - n.yh)]
-        return [self.remote(19 + i, t.mid, t.got_y.at[i], dev) for i, dev in enumerate(devices)]
+        return [self.remote(25 + i, t.mid, t.got_y.at[i], dev) for i, dev in enumerate(devices)]
 
     def start(self, copies):
         for c in copies:
@@ -441,21 +472,62 @@
         for c in copies:
             c.wait()
 
-    def core_start(self):
-        self.start(self.core_copies())
-
-    def core_to_first(self):
+    def early_start(self):
+        both = self.core_copies()
+        for core in range(2):
+            pl.when(self.n.core == core)(both[core].start)
+
+    def early_to_first(self):
         n, t = self.n, self.t
-        self.wait(self.core_copies())
-        for z in range(4):
-            rows = slice(144 * z, 144 * z + 144)
-            t.sum_m[z] = total(t.part[n.core, rows, :], t.got_core[rows, :]).astype(BF)
+        copies = self.core_copies()
+        tile2, tiles01, _ = self.first_copies()
+
+        @pl.when(n.core == 0)
+        def _():
+            copies[1].wait_recv()
+            for z in range(4):
+                rows = slice(144 * z, 144 * z + 144)
+                t.sum_m[z, :, 256:384] = total(t.part[0, rows, 256:384], t.got_core[rows, 256:384]).astype(BF)
+            self.start(tile2)
+            copies[0].wait_send()
+
+        @pl.when(n.core == 1)
+        def _():
+            copies[0].wait_recv()
+            for z in range(4):
+                rows = slice(144 * z, 144 * z + 144)
+                t.sum_m[z] = total(t.part[1, rows, :], t.got_core[rows, :]).astype(BF)
+            self.start(tile2 + tiles01)
+            copies[1].wait_send()
+
+    def late_start(self):
+        copies = self.core_copies()
+        pl.when(self.n.core == 1)(copies[3].start)
+        copies[2].start()
+
+    def late_to_first(self):
+        n, t = self.n, self.t
+        copies = self.core_copies()
+        _, tiles01, other = self.first_copies()
+
+        @pl.when(n.core == 0)
+        def _():
+            copies[3].wait_recv()
+            for z in range(4):
+                rows = slice(144 * z, 144 * z + 144)
+                t.sum_m[z, :, 0:256] = total(t.part[0, rows, 0:256], t.got_core[rows, 0:256]).astype(BF)
+            self.start(tiles01)
+
+        copies[2].wait_recv()
         t.sum_o[...] = total(t.part[n.core, 576:816, :], t.got_core[576:816, :]).astype(BF)
-        self.start(self.first_copies())
+        self.start(other)
+        copies[2].wait_send()
+        pl.when(n.core == 1)(copies[3].wait_send)
 
     def first_to_second(self):
         n, t = self.n, self.t
-        self.wait(self.first_copies())
+        for copies in self.first_copies():
+            self.wait(copies)
         t.sum_x[...] = total(t.sum_m[:, pl.ds(al(32 * n.x), 48), 128:384], *[t.got_x[i] for i in range(3)]).astype(BF)
         t.sum_zo[...] = total(t.sum_o[pl.ds(al(z_row(n.core, n.z)), 80), :], *[t.got_o[i] for i in range(3)]).astype(BF)
         t.sum_z[...] = total(t.sum_m[n.z, :, 0:128], *[t.got_z[i] for i in range(3)]).astype(BF)
@@ -519,7 +591,7 @@
     ("lbias", (3, BROWS, WT), F32), ("db_pair", (2, BROWS, WT), F32), ("parts", (32, 1, 128), F32), ("own", (2, 80, 256), F32),
     ("cot_src", (NR, 256), BF), ("cot_dst", (NR, 256), BF), ("mid_src", (NR, 256), BF), ("mid_dst", (NR, 256), BF), ("back_src", (NR, 256), BF), ("back_dst", (NR, 256), BF),
 ]
-SEMS = 15 + 44 + 31
+SEMS = 15 + 56 + 31
 
 
 def place(nlat, nlon):
@@ -613,7 +685,17 @@
 
     ex_cot.finish()
     two.dout[...] = shuffle(two.to_slots[...], two.cot_dst[:, 0:C])
-    backward_windows(two, 1, dbias_two)
+    red_one = Reduce(n, one, *sems, 15)
+    red_two = Reduce(n, two, *sems, 43)
+
+    def only_reducing(act):
+        if reduce:
+            act()
+
+    backward_feed(two, 1)
+    products_early(two)
+    only_reducing(red_two.early_start)
+    backward_attention(two, 1, dbias_two, red_two.early_to_first if reduce else None)
     two.back_src[:, 0:C] = shuffle(two.from_slots[...], two.dx[...])
     ex_back.start()
     for group in range(2):
@@ -624,32 +706,30 @@
                 two.db_pair[group, rows, :] = polar_back(two.db_pair[group, rows, :], group == 1)
 
     two.db[0:BROWS, :] = two.db_pair[0] + two.db_pair[1]
-    weight_products(two, two.part)
-    other_rows(two, two.part)
-    red_one = Reduce(n, one, *sems, 15)
-    red_two = Reduce(n, two, *sems, 37)
-    if reduce:
-        red_two.core_start()
+    products_late(two)
+    other_rows(two)
+    only_reducing(red_two.late_start)
 
     ex_back.finish()
-    if reduce:
-        red_two.core_to_first()
+    only_reducing(red_two.late_to_first)
     one.dout[...] = shuffle(one.win_send[...], one.back_dst[:, 0:C])
     one.db[...] = jnp.zeros((OROWS, WT), F32)
 
     def dbias_one(w, h, ds):
         one.db[h * WT:h * WT + WT, :] += ds
 
-    backward_windows(one, 0, dbias_one)
-    weight_products(one, one.part)
-    other_rows(one, one.part)
-    if reduce:
-        red_one.core_start()
+    backward_feed(one, 0)
+    products_early(one)
+    only_reducing(red_one.early_start)
+    backward_attention(one, 0, dbias_one, red_one.early_to_first if reduce else None)
+    products_late(one)
+    other_rows(one)
+    only_reducing(red_one.late_start)
     r["gtok"][...] = shuffle(one.to_nat[...], one.dx[...])
     if not reduce:
         return
     red_two.first_to_second()
-    red_one.core_to_first()
+    red_one.late_to_first()
     red_two.second_to_third()
     two_final = red_two.finish()
     squares = group_squares(n, two_final)
@@ -660,7 +740,7 @@
     parts = one.parts
     parts[0] = jnp.broadcast_to(squares + group_squares(n, one_final), (1, 128))
     copies = [
-        pltpu.make_async_remote_copy(src_ref=parts.at[0], dst_ref=parts.at[1 + i], send_sem=sems[0].at[59 + i], recv_sem=sems[1].at[59 + i], device_id=d, device_id_type=MESH)
+        pltpu.make_async_remote_copy(src_ref=parts.at[0], dst_ref=parts.at[1 + i], send_sem=sems[0].at[71 + i], recv_sem=sems[1].at[71 + i], device_id=d, device_id_type=MESH)
         for i, d in enumerate(level_dev)
     ]
     for c in copies:
@@ -702,12 +782,17 @@
 
 
 def copy_out(*refs):
-    half = len(OUTPUTS)
-    copies = [pltpu.make_async_copy(refs[i], refs[half + i], refs[2 * half].at[i]) for i in range(half)]
-    for c in copies:
+    k = len(OUTPUTS)
+    sem = refs[3 * k]
+    loads = [pltpu.make_async_copy(refs[i], refs[2 * k + i], sem.at[i]) for i in range(k)]
+    stores = [pltpu.make_async_copy(refs[2 * k + i], refs[k + i], sem.at[k + i]) for i in range(k)]
+    for c in loads:
         c.start()
-    for c in copies:
+    for c, d in zip(loads[::-1], stores[::-1]):
         c.wait()
+        d.start()
+    for d in stores:
+        d.wait()
 
 
 def run_copy_out(results):
@@ -717,7 +802,7 @@
         in_specs=[anywhere] * len(results),
         out_specs=[anywhere] * len(results),
         out_shape=[jax.ShapeDtypeStruct(s, d) for _, s, d in OUTPUTS],
-        scratch_shapes=[pltpu.SemaphoreType.DMA((len(OUTPUTS),))],
+        scratch_shapes=[pltpu.VMEM(s, d) for _, s, d in OUTPUTS] + [pltpu.SemaphoreType.DMA((2 * len(OUTPUTS),))],
         name="copy_out",
     )(*results)
 

time: 89.1 us -> 77.9 us (0.87)
  Pallas kernels: 88.2 us -> 77 us
    pallas_call x1, Pallas kernels: 11.4 us -> 1.73 us  [run_copy_out(): pl.pallas_call(copy_out, in_specs=[anywhere] * len(results), out_specs=[a...]
    pallas_call x1, Pallas kernels: 76.7 us -> 75.2 us  [run(): pl.pallas_call(functools.partial(kernel, nlat, nlon, reduce), in_specs=[a...]
where the time goes in v6:
time: 77.9 us; the launch traced here: 77.8 us
  Pallas kernels  77 us (99%)
  between operations  0.82 us (1%)
    pallas_call x1, Pallas kernels, run(): pl.pallas_call(functools.partial(kernel, nlat, nlon, reduce), in_specs=[a...  75.2 us
    pallas_call x1, Pallas kernels, run_copy_out(): pl.pallas_call(copy_out, in_specs=[anywhere] * len(results), out_specs=[a...  1.73 us

profile of v6, /device:TPU:1, one launch (start us, length us, event | category | flops | bytes accessed | tf_op | source)
XLA Modules:
  0.0 77.8 jit_solution(10540069883815517752)
XLA Ops:
  0.6 75.2 %two_blocks.1 = (bf16[576,192]{1,0:T(8,128)(2,1)}, f32[18,2,192]{2,1,0:T(2,128)}, f32[2,975]{1,0:T(2,128)}) custom-call(bf16[576,192]{1,0:T(8,128)(2,1)} %bitcast.8, bf16[576,192]{1,0:T(8,128)(2,1)} %bitcast.9, f32[2,2,192]{2,1,0:T(2,128)} %refs_2_.1, bf16[2,192,576]{2,1,0:T(8,128)(2,1)} %refs_3_.1, bf16[2,192,192]{2,1,0:T(8,128)(2,1)} %refs_4_.1, ...), custom_call_target="tpu_custom_call" | custom-call | tf_op jit(solution)/shard_map/two_blocks/pallas_call | solution.py:772
  75.9 1.7 %copy_out.1 = (bf16[576,192]{1,0:T(8,128)(2,1)}, f32[18,2,192]{2,1,0:T(2,128)}, f32[2,975]{1,0:T(2,128)}) custom-call(bf16[576,192]{1,0:T(8,128)(2,1)} %get-tuple-element.9.refs_0_, f32[18,2,192]{2,1,0:T(2,128)} %get-tuple-element.10.refs_1_, f32[2,975]{1,0:T(2,128)} %get-tuple-element.11.refs_2_), custom_call_target="tpu_custom_call" | custom-call | tf_op jit(solution)/shard_map/copy_out/pallas_call | solution.py:800

commit v7 on v6

--- a/solution.py
+++ b/solution.py
@@ -614,7 +614,15 @@
 def kernel(nlat, nlon, reduce, *refs):
     names = INPUTS + [o[0] for o in OUTPUTS] + ["first_" + e[0] for e in BLOCK] + ["second_" + e[0] for e in BLOCK] + [e[0] for e in SHARED] + ["in_" + k for k in COPIED] + ["send_sem", "recv_sem", "in_sem"]
     r = dict(zip(names, refs, strict=True))
-    loads = {k: pltpu.make_async_copy(r[k], r["in_" + k], r["in_sem"].at[i]) for i, k in enumerate(COPIED)}
+    loads = {}
+    for i, k in enumerate(COPIED):
+        src, dst = r[k], r["in_" + k]
+        if k == "bias":
+            loads["bias"] = pltpu.make_async_copy(src.at[0], dst.at[0], r["in_sem"].at[i])
+        else:
+            loads[k] = pltpu.make_async_copy(src, dst, r["in_sem"].at[i])
+        if k == "w_down":
+            loads["bias_two"] = pltpu.make_async_copy(r["bias"].at[1], r["in_bias"].at[1], r["in_sem"].at[len(COPIED)])
     for copy in loads.values():
         copy.start()
 
@@ -660,7 +668,7 @@
     need("send_nat", "cot")
     one.cot_src[:, 0:C] = shuffle(one.send_nat[...], one.cot[...])
     ex_cot.start()
-    need("to_slots", "from_slots", "win_send", "to_nat")
+    need("bias_two", "to_slots", "from_slots", "win_send", "to_nat")
 
     for group in range(2):
         polar = n.first if group == 0 else n.last
@@ -721,16 +729,20 @@
     backward_feed(one, 0)
     products_early(one)
     only_reducing(red_one.early_start)
-    backward_attention(one, 0, dbias_one, red_one.early_to_first if reduce else None)
+
+    def middle():
+        red_two.first_to_second()
+        red_one.early_to_first()
+
+    backward_attention(one, 0, dbias_one, middle if reduce else None)
     products_late(one)
     other_rows(one)
     only_reducing(red_one.late_start)
     r["gtok"][...] = shuffle(one.to_nat[...], one.dx[...])
     if not reduce:
         return
-    red_two.first_to_second()
+    red_two.second_to_third()
     red_one.late_to_first()
-    red_two.second_to_third()
     two_final = red_two.finish()
     squares = group_squares(n, two_final)
     red_one.first_to_second()
@@ -775,7 +787,7 @@
         out_specs=[vmem] * len(OUTPUTS),
         out_shape=[jax.ShapeDtypeStruct(s, d) for _, s, d in OUTPUTS],
         scratch_shapes=[pltpu.VMEM(s, d) for _, s, d in BLOCK + BLOCK + SHARED] + [pltpu.VMEM(SHAPES[k], F32 if k == "bias" else BF) for k in COPIED]
-        + [pltpu.SemaphoreType.DMA((SEMS,))] * 2 + [pltpu.SemaphoreType.DMA((len(COPIED),))],
+        + [pltpu.SemaphoreType.DMA((SEMS,))] * 2 + [pltpu.SemaphoreType.DMA((len(COPIED) + 1,))],
         compiler_params=pltpu.CompilerParams(vmem_limit_bytes=VMEM_LIMIT, collective_id=1, has_side_effects=True),
         name="two_blocks",
     )(*args)

time: 77.9 us -> 75.9 us (0.974)
  Pallas kernels: 77 us -> 75 us
    pallas_call x1, Pallas kernels: 75.2 us -> 73.2 us  [run(): pl.pallas_call(functools.partial(kernel, nlat, nlon, reduce), in_specs=[a...]
where the time goes in v7:
time: 75.9 us; the launch traced here: 75.8 us
  Pallas kernels  75 us (99%)
  between operations  0.82 us (1%)
    pallas_call x1, Pallas kernels, run(): pl.pallas_call(functools.partial(kernel, nlat, nlon, reduce), in_specs=[a...  73.2 us
    pallas_call x1, Pallas kernels, run_copy_out(): pl.pallas_call(copy_out, in_specs=[anywhere] * len(results), out_specs=[a...  1.73 us

profile of v7, /device:TPU:1, one launch (start us, length us, event | category | flops | bytes accessed | tf_op | source)
XLA Modules:
  0.0 75.8 jit_solution(4911061254998807505)
XLA Ops:
  0.6 73.2 %two_blocks.1 = (bf16[576,192]{1,0:T(8,128)(2,1)}, f32[18,2,192]{2,1,0:T(2,128)}, f32[2,975]{1,0:T(2,128)}) custom-call(bf16[576,192]{1,0:T(8,128)(2,1)} %bitcast.8, bf16[576,192]{1,0:T(8,128)(2,1)} %bitcast.9, f32[2,2,192]{2,1,0:T(2,128)} %refs_2_.1, bf16[2,192,576]{2,1,0:T(8,128)(2,1)} %refs_3_.1, bf16[2,192,192]{2,1,0:T(8,128)(2,1)} %refs_4_.1, ...), custom_call_target="tpu_custom_call" | custom-call | tf_op jit(solution)/shard_map/two_blocks/pallas_call | solution.py:784
  73.9 1.7 %copy_out.1 = (bf16[576,192]{1,0:T(8,128)(2,1)}, f32[18,2,192]{2,1,0:T(2,128)}, f32[2,975]{1,0:T(2,128)}) custom-call(bf16[576,192]{1,0:T(8,128)(2,1)} %get-tuple-element.9.refs_0_, f32[18,2,192]{2,1,0:T(2,128)} %get-tuple-element.10.refs_1_, f32[2,975]{1,0:T(2,128)} %get-tuple-element.11.refs_2_), custom_call_target="tpu_custom_call" | custom-call | tf_op jit(solution)/shard_map/copy_out/pallas_call | solution.py:812

commit v8 on v7

--- a/solution.py
+++ b/solution.py
@@ -741,8 +741,8 @@
     r["gtok"][...] = shuffle(one.to_nat[...], one.dx[...])
     if not reduce:
         return
+    red_one.late_to_first()
     red_two.second_to_third()
-    red_one.late_to_first()
     two_final = red_two.finish()
     squares = group_squares(n, two_final)
     red_one.first_to_second()

time: 75.9 us -> 75.5 us (level)
  no operation moved by 1% of the time
where the time goes in v8:
time: 75.5 us; the launch traced here: 75.3 us
  Pallas kernels  74.5 us (99%)
  between operations  0.82 us (1%)
    pallas_call x1, Pallas kernels, run(): pl.pallas_call(functools.partial(kernel, nlat, nlon, reduce), in_specs=[a...  72.8 us
    pallas_call x1, Pallas kernels, run_copy_out(): pl.pallas_call(copy_out, in_specs=[anywhere] * len(results), out_specs=[a...  1.73 us

profile of v8, /device:TPU:1, one launch (start us, length us, event | category | flops | bytes accessed | tf_op | source)
XLA Modules:
  0.0 75.3 jit_solution(11764711951286778632)
XLA Ops:
  0.6 72.8 %two_blocks.1 = (bf16[576,192]{1,0:T(8,128)(2,1)}, f32[18,2,192]{2,1,0:T(2,128)}, f32[2,975]{1,0:T(2,128)}) custom-call(bf16[576,192]{1,0:T(8,128)(2,1)} %bitcast.8, bf16[576,192]{1,0:T(8,128)(2,1)} %bitcast.9, f32[2,2,192]{2,1,0:T(2,128)} %refs_2_.1, bf16[2,192,576]{2,1,0:T(8,128)(2,1)} %refs_3_.1, bf16[2,192,192]{2,1,0:T(8,128)(2,1)} %refs_4_.1, ...), custom_call_target="tpu_custom_call" | custom-call | tf_op jit(solution)/shard_map/two_blocks/pallas_call | solution.py:784
  73.4 1.7 %copy_out.1 = (bf16[576,192]{1,0:T(8,128)(2,1)}, f32[18,2,192]{2,1,0:T(2,128)}, f32[2,975]{1,0:T(2,128)}) custom-call(bf16[576,192]{1,0:T(8,128)(2,1)} %get-tuple-element.9.refs_0_, f32[18,2,192]{2,1,0:T(2,128)} %get-tuple-element.10.refs_1_, f32[2,975]{1,0:T(2,128)} %get-tuple-element.11.refs_2_), custom_call_target="tpu_custom_call" | custom-call | tf_op jit(solution)/shard_map/copy_out/pallas_call | solution.py:812
